TPU v7x, 512 devices: a whole 4x4x16 slice. The times are simulated.
512 devices in a mesh: dp: 32 (over z, core), tensor: 16 (over y, x).
Axes of the slice: x: 4, y: 4, z: 16, core: 2. Of those that a mesh axis runs over, the one named last changes fastest.
Arguments:
- responses: bfloat16 [32, 1280, 4608], P('dp', 'tensor'), may hold values from -6 to 6
- kl_terms: bfloat16 [32, 8, 160], P('dp'), may hold values from -3 to 3
- norm_gain: float32 [4608], replicated, may hold values from 0.5 to 1.5
- w_qkv: bfloat16 [4608, 16, 384], P(None, 'tensor'), may hold values from -0.20623948 to 0.20623948
- readout: bfloat16 [16, 128], P('tensor'), may hold values from -0.5 to 0.5
- slot_bin: int32 [32, 8], P('dp'), may hold values from 0 to 31, as said below
- entry_source: int32 [32, 8], P('dp'), may hold values from 0 to 31, as said below
- bin_segments: int32 [32, 64], P('dp'), may hold values from 0 to 7, never falling along the last dimension, each value on 1 to 10 neighbouring positions
Outputs:
- head_outputs: bfloat16 [32, 1024, 2048], P('dp', None, 'tensor')
- scores: float32 [32, 8], P('dp')
Inputs may be any that keep to these rules, and one draw needn't show every extreme that they name: Slot j of group g becomes entry j of bin slot_bin[g, j]; the slots of one group go to distinct bins. Entry j of bin b is slot j of group entry_source[b, j]; the entries of one bin come from distinct groups; slot_bin[entry_source[b, j], j] == b.
All inputs are finite; a program needn't handle non-finite values.
Results may differ from a plain program's by a relative error of at most 0.006.
The roundings to bfloat16 on the way count: a program that leaves them out, or rounds other values in their place, can miss the bound.
Values may be sent and summed in bfloat16 or wider, within the bound.
A program may use at most 64 MiB of HBM per device.

v0:
```python
import jax
import jax.numpy as jnp
from jax import lax
from jax.sharding import PartitionSpec as P

D = 4608
HD = 128
RESP = 8
CAP = 10
BIN_DEV = 64


epsilon = 1e-06
beta_weight = 0.05
score_scale = 1.0 / 12.0
soft_cap = 50.0
rope_base = 10000.0


def rms_scaled(features, gain_vec):
    widened = features.astype(jnp.float32)
    mean_square = jnp.mean(widened * widened, axis=-1, keepdims=True)
    return (widened * lax.rsqrt(mean_square + epsilon) * gain_vec).astype(jnp.bfloat16)


def rotate(heads_block, positions):
    halfway = heads_block.shape[-1] // 2
    frequency = rope_base ** (-2.0 * jnp.arange(halfway, dtype=jnp.float32) / heads_block.shape[-1])
    angles = positions.astype(jnp.float32)[:, None] * frequency[None, :]
    cosine = jnp.cos(angles)[:, None, :]
    sine_part = jnp.sin(angles)[:, None, :]
    widened = heads_block.astype(jnp.float32)
    first_half = widened[..., :halfway]
    second = widened[..., halfway:]
    joined = jnp.concatenate(
        [first_half * cosine - second * sine_part, second * cosine + first_half * sine_part],
        axis=-1,
    )
    return joined.astype(jnp.bfloat16)


def attend(queries, keys_rot, values, allowed):
    logits = (
        jnp.einsum("qd,kd->qk", queries, keys_rot, preferred_element_type=jnp.float32) * score_scale
    )
    capped = soft_cap * jnp.tanh(logits / soft_cap)
    expo = jnp.where(allowed, jnp.exp(capped), 0.0)
    probs = (expo / jnp.sum(expo, axis=-1, keepdims=True)).astype(jnp.bfloat16)
    return jnp.dot(probs, values, preferred_element_type=jnp.float32).astype(jnp.bfloat16)


def body(responses, kl_terms, norm_gain, w_qkv, readout, slot_bin, entry_source, bin_segments):
    groups = lax.axis_size("dp")
    pieces = lax.axis_size("tensor")
    local_heads = w_qkv.shape[1]
    head_width = local_heads * 3 * HD
    weights = w_qkv.reshape(D, head_width)
    segments = bin_segments[0]
    seg_onehot = (segments[:, None] == jnp.arange(RESP, dtype=jnp.int32)[None, :]).astype(jnp.int32)
    piece_rows = jnp.sum(seg_onehot, axis=0)
    offsets = jnp.cumsum(piece_rows) - piece_rows
    within = jnp.arange(BIN_DEV, dtype=jnp.int32) - jnp.sum(seg_onehot * offsets[None, :], axis=1)
    row_source = jnp.sum(seg_onehot * entry_source[0][None, :], axis=1)
    row_length = jnp.sum(seg_onehot * piece_rows[None, :], axis=1)
    flat_index = row_source * CAP + within
    target = (slot_bin[0][None, :] == jnp.arange(groups, dtype=jnp.int32)[:, None]).astype(
        jnp.bfloat16
    )
    send_kl = jnp.einsum(
        "gj,js->gs", target, kl_terms[0], preferred_element_type=jnp.float32
    ).astype(jnp.bfloat16)
    slots = responses[0].reshape(RESP, CAP, D)
    send_rows = jnp.einsum("gj,jcd->gcd", target, slots, preferred_element_type=jnp.float32).astype(
        jnp.bfloat16
    )
    recv_rows, recv_kl = (
        lax.all_to_all(send_rows, "dp", split_axis=0, concat_axis=0, tiled=True),
        lax.all_to_all(send_kl, "dp", split_axis=0, concat_axis=0, tiled=True),
    )
    entry_kl = recv_kl[entry_source[0]].astype(jnp.float32)
    packed = recv_rows.reshape(groups * CAP, D)[flat_index]
    normed = rms_scaled(packed, norm_gain)
    raw_heads = jnp.dot(
        lax.all_gather(normed, "tensor", axis=0, tiled=True),
        weights,
        preferred_element_type=jnp.float32,
    ).astype(jnp.bfloat16)
    raw_heads = raw_heads.reshape(pieces * BIN_DEV, local_heads, 3, HD)
    piece_ids = jnp.arange(pieces, dtype=jnp.int32)
    positions = (piece_ids[:, None] * row_length[None, :] + within[None, :]).reshape(-1)
    all_segments = jnp.tile(segments, pieces)
    queries = rotate(raw_heads[:, :, 0], positions)
    keys_rot = rotate(raw_heads[:, :, 1], positions)
    values = raw_heads[:, :, 2]
    allowed = (all_segments[:, None] == all_segments[None, :]) & (
        positions[None, :] <= positions[:, None]
    )
    outputs = [attend(queries[:, 0], keys_rot[:, 0], values[:, 0], allowed)]
    head_rows = jnp.stack(outputs, axis=1)
    last_rows = (pieces - 1) * BIN_DEV + offsets + piece_rows - 1
    picked = head_rows[last_rows].astype(jnp.float32)
    reward_part = jnp.sum(picked * readout.astype(jnp.float32)[None, :, :], axis=(1, 2))
    summed = lax.psum(reward_part, "tensor")
    tokens = jnp.arange(entry_kl.shape[1], dtype=jnp.int32)
    live_tokens = tokens[None, :] < (piece_rows * pieces)[:, None]
    penalty = jnp.sum(jnp.where(live_tokens, entry_kl, 0.0), axis=1)
    scores = (summed - beta_weight * penalty)[None, :]
    return (head_rows.reshape(1, pieces * BIN_DEV, local_heads * HD), scores)


def solution(mesh):
    placed = (
        P("dp", "tensor", None),
        P("dp", None, None),
        P(),
        P(None, "tensor", None),
        P("tensor", None),
        P("dp", None),
        P("dp", None),
        P("dp", None),
    )
    return jax.shard_map(
        body,
        mesh=mesh,
        in_specs=placed,
        out_specs=(P("dp", None, "tensor"), P("dp", None)),
        check_vma=False,
    )
```

profile of v0, /device:TPU:6, one launch (start us, length us, event | category | flops | bytes accessed | tf_op | source)
XLA Modules:
  0.0 395.1 jit_solution(16604992815069227812)
XLA Ops:
  7.2 0.0 copy-start
  7.2 2.5 reshape_squeeze.3
  9.7 2.5 convolution_convert_fusion
  12.2 3.9 copy.20
  16.1 15.7 %all-to-all-start = ((bf16[32,10,4608]{2,1,0:T(8,128)(2,1)}), bf16[32,10,4608]{2,1,0:T(8,128)(2,1)}, u32[]{:S(2)}, u32[]{:S(2)}) async-start(bf16[32,10,4608]{2,1,0:T(8,128)(2,1)} %copy.20), calls=%async_computation | async-start | bytes 9437184 | tf_op jit(solution)/shard_map/all_to_all | solution.py:77
  31.8 0.0 all-gather.2.cloned.1.call-start
  31.9 0.1 convert_reduce_fusion
  32.0 0.2 reduce-window.4
  32.2 0.5 broadcast_multiply_fusion
  32.7 0.1 select_reduce_fusion.3
  32.8 0.5 copy-done.10
  33.4 203.3 %all-to-all-done = bf16[32,10,4608]{2,1,0:T(8,128)(2,1)} async-done(((bf16[32,10,4608]{2,1,0:T(8,128)(2,1)}), bf16[32,10,4608]{2,1,0:T(8,128)(2,1)}, u32[]{:S(2)}, u32[]{:S(2)}) %all-to-all-start) | async-done | bytes 2949152 | tf_op jit(solution)/shard_map/all_to_all | solution.py:77
  236.6 4.9 %reshape.378 = bf16[320,4608]{1,0:T(8,128)(2,1)} reshape(bf16[32,10,4608]{2,1,0:T(8,128)(2,1)} %all-to-all-done) | data formatting | bytes 5898240 | tf_op jit(solution)/shard_map/reshape | solution.py:81
  241.5 4.5 %gather_fusion = bf16[64,4608]{1,0:T(8,128)(2,1)} fusion(bf16[320,4608]{1,0:T(8,128)(2,1)} %reshape.378, s32[1024]{0:T(1024)S(1)} %pad_clamp_fusion.2), kind=kCustom, calls=%fused_computation | custom fusion | bytes 1179904 | tf_op jit(solution)/shard_map/gather | solution.py:81
  246.0 1.3 fusion.8
  247.3 2.1 fusion.10
  249.4 0.0 all-gather.2.cloned.1.call-update
  249.4 1.0 fusion.11
  250.4 0.6 copy.21
  251.0 11.6 %all-to-all-start.1 = ((bf16[32,1,160]{2,1,0:T(2,128)(2,1)}), bf16[32,1,160]{2,1,0:T(2,128)(2,1)}, u32[]{:S(2)}, u32[]{:S(2)}) async-start(bf16[32,1,160]{2,1,0:T(2,128)(2,1)} %copy.21), calls=%async_computation.1 | async-start | bytes 65536 | tf_op jit(solution)/shard_map/all_to_all | solution.py:78
  262.6 0.6 fusion.49
  263.2 0.6 pad_clamp_fusion.1
  263.8 0.7 fusion.50
  264.5 0.6 pad_clamp_fusion
  265.1 0.6 iota_subtract_fusion
  265.7 1.2 bitcast_convert_fusion
  266.9 0.6 multiply_power_fusion
  267.5 0.1 add.119
  267.5 0.6 convert_element_type.95
  268.1 0.7 eq.43
  268.8 6.5 %all-to-all-done.1 = bf16[32,1,160]{2,1,0:T(2,128)(2,1)} async-done(((bf16[32,1,160]{2,1,0:T(2,128)(2,1)}), bf16[32,1,160]{2,1,0:T(2,128)(2,1)}, u32[]{:S(2)}, u32[]{:S(2)}) %all-to-all-start.1) | async-done | bytes 10272 | tf_op jit(solution)/shard_map/all_to_all | solution.py:78
  275.3 0.8 copy.26
  276.0 1.3 gather_fusion.2
  277.3 63.5 %all-gather.2.cloned.1.call-done = bf16[1024,4608]{1,0:T(8,128)(2,1)} async-done(((bf16[64,4608]{1,0:T(8,128)(2,1)}), bf16[1024,4608]{1,0:T(8,128)(2,1)}) %all-gather.2.cloned.1.call-update) | async-done | bytes 9437200 | tf_op jit(solution)/shard_map/all_gather | solution.py:84
  340.8 6.5 %fusion.4 = bf16[1024,384]{0,1:T(8,128)(2,1)S(1)} fusion(bf16[1024,4608]{1,0:T(8,128)(2,1)} %all-gather.2.cloned.1.call-done, bf16[4608,1,384]{2,0,1:T(8,128)(2,1)S(1)} %copy-done), kind=kOutput, calls=%fused_computation.12 | convolution fusion | flops 3624271872 | bytes 13762560 | tf_op jit(solution)/shard_map/dot_general | solution.py:83
  347.4 0.1 fusion.29
  347.5 1.2 fusion.39
  348.7 0.0 copy-done.4
  348.7 0.0 copy-done.5
  348.7 1.7 fusion.2
  350.4 0.0 copy-start.2
  350.4 0.0 copy-start.7
  350.4 2.6 fusion.7
  353.0 1.7 gather_fusion.1
  354.7 0.7 fusion.42
  355.5 0.2 select_reduce_fusion
  355.6 32.1 %psum.7 = f32[8]{0:T(128)S(1)} all-reduce(f32[8]{0:T(128)S(1)} %fusion.42), channel_id=1, replica_groups=mesh['dp'=32,'tensor'=16] {'tensor'}, use_global_device_ids=true, to_apply=%region_8.9 | all-reduce | flops 8 | bytes 64 | tf_op jit(solution)/shard_map/psum | solution.py:103
  387.7 0.5 subtract_bitcast_fusion
  (23 shorter events, 0.1 us)
Async XLA Ops:
  7.2 333.6 %copy-start = (bf16[4608,1,384]{2,0,1:T(8,128)(2,1)S(1)}, bf16[4608,1,384]{2,0,1:T(8,128)(2,1)}, u32[]{:S(2)}) copy-start(bf16[4608,1,384]{2,0,1:T(8,128)(2,1)} %param.11) | copy-start | bytes 10616836
  16.1 15.8 %copy-start.6 = (s32[1,64]{1,0:T(1,128)S(1)}, s32[1,64]{1,0:T(1,128)}, u32[]{:S(2)}) copy-start(s32[1,64]{1,0:T(1,128)} %param.15) | copy-start | bytes 772
  16.1 16.6 %copy-start.9 = (s32[1,8]{1,0:T(1,128)S(1)}, s32[1,8]{1,0:T(1,128)}, u32[]{:S(2)}) copy-start(s32[1,8]{1,0:T(1,128)} %param.14) | copy-start | bytes 100
  16.1 220.5 %all-to-all-start = ((bf16[32,10,4608]{2,1,0:T(8,128)(2,1)}), bf16[32,10,4608]{2,1,0:T(8,128)(2,1)}, u32[]{:S(2)}, u32[]{:S(2)}) async-start(bf16[32,10,4608]{2,1,0:T(8,128)(2,1)} %copy.20), calls=%async_computation | async-start | bytes 9437184 | tf_op jit(solution)/shard_map/all_to_all | solution.py:77
  31.8 309.0 %all-gather.2.cloned.1.call-start = ((), (), s32[]{:S(2)}) async-start(), calls=%async_computation.2 | async-start | bytes 10027008 | tf_op jit(solution)/shard_map/all_gather | solution.py:84
  32.2 0.5 copy-start.11
  32.8 0.5 copy-start.10
  251.0 24.2 %all-to-all-start.1 = ((bf16[32,1,160]{2,1,0:T(2,128)(2,1)}), bf16[32,1,160]{2,1,0:T(2,128)(2,1)}, u32[]{:S(2)}, u32[]{:S(2)}) async-start(bf16[32,1,160]{2,1,0:T(2,128)(2,1)} %copy.21), calls=%async_computation.1 | async-start | bytes 65536 | tf_op jit(solution)/shard_map/all_to_all | solution.py:78
  267.5 1.3 copy-start.3
  277.3 70.2 %copy-start.1 = (f32[1024]{0:T(1024)S(1)}, f32[1024]{0:T(1024)}, u32[]{:S(2)}) copy-start(f32[1024]{0:T(1024)} %convert_element_type.95) | copy-start | bytes 12292
  277.3 70.2 %copy-start.8 = (f32[64]{0:T(128)S(1)}, f32[64]{0:T(128)}, u32[]{:S(2)}) copy-start(f32[64]{0:T(128)} %multiply_power_fusion) | copy-start | bytes 772
  277.3 71.4 %copy-start.4 = (s32[1024]{0:T(1024)S(1)}, s32[1024]{0:T(1024)}, u32[]{:S(2)}) copy-start(s32[1024]{0:T(1024)} %copy-done.3) | copy-start | bytes 12292
  277.3 71.4 %copy-start.5 = (s32[1024]{0:T(1024)S(1)}, s32[1024]{0:T(1024)}, u32[]{:S(2)}) copy-start(s32[1024]{0:T(1024)} %eq.43) | copy-start | bytes 12292
  350.4 5.1 %copy-start.2 = (bf16[8,160]{1,0:T(8,128)(2,1)S(1)}, bf16[8,160]{1,0:T(8,128)(2,1)}, u32[]{:S(2)}) copy-start(bf16[8,160]{1,0:T(8,128)(2,1)} %gather_fusion.2) | copy-start | bytes 7684
  350.4 5.0 %copy-start.7 = (s32[8]{0:T(128)S(1)}, s32[8]{0:T(128)}, u32[]{:S(2)}) copy-start(s32[8]{0:T(128)} %get-tuple-element.13) | copy-start | bytes 100
Sparse Core Ops, SparseCore 0:
  249.6 91.1 all-gather.1
where the time goes:
time: 402 us; the launch traced here: 395 us
  waiting for transfers between devices  273 us (68%)
  blocking collectives  32.1 us (8%)
  starting transfers between devices  27.3 us (7%)
  local copies, waits for them, and re-layouts  21.5 us (5%)
  matrix products  14.3 us (4%)
  between operations  14.2 us (4%)
  other arithmetic  12.5 us (3%)
    all_to_all x1, waiting for transfers between devices, body(): lax.all_to_all(send_rows, 'dp', split_axis=0, concat_axis=0, tiled=True)  203 us
    all_gather x1, waiting for transfers between devices, body(): lax.all_gather(normed, 'tensor', axis=0, tiled=True)  63.5 us
    psum x1, blocking collectives, body(): summed = lax.psum(reward_part, 'tensor')  32.1 us
    all_to_all x1, starting transfers between devices, body(): lax.all_to_all(send_rows, 'dp', split_axis=0, concat_axis=0, tiled=True)  15.7 us
    all_to_all x1, starting transfers between devices, body(): lax.all_to_all(send_kl, 'dp', split_axis=0, concat_axis=0, tiled=True)  11.6 us
  transfers between devices with their start and end apart: 3, of which 3 were waited for; matrix products, arithmetic and copies ran while one was open for 3% of the time, Pallas kernels for 0%

commit v1 on v0

v1 whole, which is shorter than its diff:
```python
import jax
import jax.numpy as jnp
import numpy as np
from jax import lax
from jax.experimental import pallas as pl
from jax.experimental.pallas import tpu as pltpu
from jax.sharding import PartitionSpec as P

D = 4608
HALF_D = D // 2
HD = 128
RESP = 8
CAP = 10
BIN_DEV = 64
LMAX = 160
PIECES = 16
NZ = 16
CHUNK = 16
CHUNKS = 5
ROWS = PIECES * CHUNK
ROWS_DEV = 80

epsilon = 1e-06
beta_weight = 0.05
score_scale = 1.0 / 12.0
soft_cap = 50.0
rope_base = 10000.0

F32 = jnp.float32
BF16 = jnp.bfloat16
I32 = jnp.int32


def iota(shape, dim):
    return lax.broadcasted_iota(I32, shape, dim)


def slot_of(row):
    slot = jnp.zeros_like(row)
    for j in range(1, RESP):
        slot = slot + jnp.where(row >= CAP * j, 1, 0)
    return slot


def per_slot(slot, counts):
    out = jnp.zeros(slot.shape, I32)
    for j in range(RESP):
        out = jnp.where(slot == j, counts[j], out)
    return out


def kernel(
    resp, kl, gain, freq, w_hbm, readout, slot_bin, entry_source, bin_segments,
    out, scores,
    gath, w, meta, cos_t, sin_t, qs, ks, vs, os, zb, sel0, sel1, ob, rx, ry, sc,
    w_sem, r1, r2, ag_send, meta_send, meta_recv, p1_send, p1_recv, sib_send, sib_recv,
    p2_send, p2_recv, rw_send, rw_recv,
):
    d = lax.axis_index("dp")
    t = lax.axis_index("tensor")
    z, core = d // 2, d % 2
    y, x = t // 4, t % 4
    a = (1 - core) * x + core * y
    b = (1 - core) * y + core * x

    def piece(i, j):
        i, j = (a + i) % 4, (b + j) % 4
        return (1 - core) * (j * 4 + i) + core * (i * 4 + j)

    def in_z(target):
        return {"dp": target * 2 + core}

    sibling = {"dp": z * 2 + (1 - core)}

    def remote(src, dst, send, recv, device):
        return pltpu.make_async_remote_copy(
            src_ref=src, dst_ref=dst, send_sem=send, recv_sem=recv,
            device_id=device, device_id_type=pl.DeviceIdType.MESH,
        )

    def drain(ref, sem):
        pltpu.make_async_copy(ref, ref, sem).wait()

    w_copy = pltpu.make_async_copy(w_hbm, w, w_sem)
    w_copy.start()
    barrier = pltpu.get_barrier_semaphore()

    def greet(device):
        pl.semaphore_signal(barrier, inc=1, device_id=device, device_id_type=pl.DeviceIdType.MESH)

    for i in range(1, 4):
        greet({"tensor": piece(i, 0)})
        greet({"tensor": piece(0, i)})
    greet(sibling)

    def greet_z(i, carry):
        greet(in_z((z + i) % NZ))
        return carry

    lax.fori_loop(1, NZ, greet_z, 0)

    lane = iota((1, HD), 1)
    meta[core, z] = jnp.full((8, HD), 99, I32)
    meta[core, z, 0:1, 0:BIN_DEV] = bin_segments[...]
    meta[core, z, 1:2, 0:RESP] = entry_source[...]

    for c in range(CHUNKS):
        rows = resp[CHUNK * c:CHUNK * (c + 1), :].astype(F32)
        mean_square = jnp.sum(rows * rows, axis=-1, keepdims=True) * (1.0 / D)
        normed = rows * lax.rsqrt(mean_square + epsilon) * gain[...]
        gath[c, t] = normed.astype(BF16)

    pl.semaphore_wait(barrier, 6 + 1 + NZ - 1)

    lo, hi = pl.ds(0, HALF_D), pl.ds(HALF_D, HALF_D)
    up_a, down_a = {"tensor": piece(1, 0)}, {"tensor": piece(-1, 0)}
    up_b, down_b = {"tensor": piece(0, 1)}, {"tensor": piece(0, -1)}
    order = (0, -1, 1, 2)

    def full(c, p, sem, device):
        return remote(gath.at[c, p], gath.at[c, p], ag_send.at[c], sem, device)

    def half(c, p, cols, sem, device):
        view = gath.at[c, p, :, cols]
        return remote(view, view, ag_send.at[c], sem, device)

    def second_sends(c, i):
        p = piece(order[i], 0)
        full(c, p, r2.at[c, i, 0], up_b).start()
        full(c, p, r2.at[c, i, 1], down_b).start()

    def first_ring(c):
        if c == 0:
            second_sends(c, 0)
        full(c, piece(-1, 0), r1.at[c, 0], up_a).wait_recv()
        half(c, piece(-1, 0), lo, r1.at[c, 2], up_a).start()
        if c > 0:
            second_sends(c, 0)
        second_sends(c, 1)
        full(c, piece(1, 0), r1.at[c, 1], down_a).wait_recv()
        half(c, piece(1, 0), hi, r1.at[c, 3], down_a).start()
        second_sends(c, 2)
        half(c, piece(2, 0), lo, r1.at[c, 2], up_a).wait_recv()
        half(c, piece(2, 0), hi, r1.at[c, 3], down_a).wait_recv()
        second_sends(c, 3)

    def second_ring(c):
        for i in range(4):
            below, above = piece(order[i], -1), piece(order[i], 1)
            full(c, below, r2.at[c, i, 0], up_b).wait_recv()
            half(c, below, lo, r2.at[c, i, 2], up_b).start()
            full(c, above, r2.at[c, i, 1], down_b).wait_recv()
            half(c, above, hi, r2.at[c, i, 3], down_b).start()

    def second_end(c):
        for i in range(4):
            opposite = piece(order[i], 2)
            half(c, opposite, lo, r2.at[c, i, 2], up_b).wait_recv()
            half(c, opposite, hi, r2.at[c, i, 3], down_b).wait_recv()

    for c in range(CHUNKS):
        full(c, t, r1.at[c, 0], up_a).start()
        full(c, t, r1.at[c, 1], down_a).start()

    def send_z(ref_of, dst, send, recv):
        def body(i, carry):
            target = (z + i) % NZ
            remote(ref_of(target), dst, send, recv, in_z(target)).start()
            return carry

        lax.fori_loop(1, NZ, body, 0)

    send_z(lambda target: meta.at[core, z], meta.at[core, z], meta_send.at[0], meta_recv.at[0])

    first_ring(0)

    drain(meta.at[core, pl.ds(0, NZ - 1)], meta_recv.at[0])
    meta_pass = remote(meta.at[core], meta.at[core], meta_send.at[1], meta_recv.at[1], sibling)
    meta_pass.start()
    remote(meta.at[1 - core], meta.at[1 - core], meta_send.at[1], meta_recv.at[1], sibling).wait_recv()

    every = meta[...].reshape(2 * NZ, 8, HD)
    tile_row = iota((2 * NZ, 8, HD), 1)
    tile_id = iota((2 * NZ, 8, HD), 0)
    tile_bin = (tile_id % NZ) * 2 + tile_id // NZ
    is_segment = tile_row == 0
    own_bins = jnp.full((1, HD), -1, I32)
    for j in range(RESP):
        own_bins = jnp.where(lane == j, slot_bin[0:1, j:j + 1], own_bins)
    counts = []
    for j in range(RESP):
        hit = is_segment & (every == j) & (tile_bin == slot_bin[0:1, j:j + 1].reshape(1, 1, 1))
        counts.append(jnp.sum(jnp.where(hit, 1.0, 0.0)).astype(I32))

    last_row = jnp.full((1, HD), -1, I32)
    penalty = jnp.zeros((1, HD), F32)
    token = iota((1, LMAX), 1)
    for j in range(RESP):
        last_row = jnp.where(lane == j, CAP * j + counts[j] - 1, last_row)
        live = jnp.where(token < counts[j] * PIECES, kl[j:j + 1, :].astype(F32), 0.0)
        penalty = jnp.where(lane == j, jnp.sum(live, axis=1, keepdims=True), penalty)

    def rope_tables(c, carry):
        index = iota((ROWS, HD), 0)
        row = CHUNK * c + index % CHUNK
        slot = slot_of(row)
        position = (index // CHUNK) * per_slot(slot, counts) + row - CAP * slot
        angle = position.astype(F32) * freq[...]
        cos_t[c] = jnp.cos(angle)
        sine = jnp.sin(angle)
        sin_t[c] = jnp.where(iota((ROWS, HD), 1) < HD // 2, -sine, sine)
        return carry

    lax.fori_loop(0, CHUNKS, rope_tables, 0)

    def pick_rows(i, carry):
        tile = meta[core, i]
        seg_row = tile[0:1, :].astype(F32)
        src_row = tile[1:2, :].astype(F32)
        r_col = iota((BIN_DEV, HD), 0)
        l_row = iota((BIN_DEV, HD), 1)
        seg = jnp.sum(jnp.where(r_col == l_row, seg_row, 0.0), axis=1, keepdims=True)
        offset = jnp.sum(jnp.where(seg_row < seg, 1.0, 0.0), axis=1, keepdims=True)
        source = jnp.sum(jnp.where(l_row.astype(F32) == seg, src_row, 0.0), axis=1, keepdims=True)
        source = source.astype(I32)
        row = CAP * seg.astype(I32) + r_col[:, 0:1] - offset.astype(I32)
        base = ((source & 1) * NZ + (source >> 1)) * 32
        late = jnp.where(row < 60, NZ * 64 + row - 32, NZ * 128 + row - 48)
        column = base + jnp.where(row < 32, row, late)
        top = iota((32, 64 * NZ * 2), 1) == column[0:32]
        sel0[i] = jnp.where(top, 1.0, 0.0).astype(BF16)
        low = iota((32, 96 * NZ * 2), 1) == column[32:64]
        sel1[i] = jnp.where(low, 1.0, 0.0).astype(BF16)
        return carry

    lax.fori_loop(0, NZ, pick_rows, 0)

    def project(c):
        raw = jnp.dot(gath[c].reshape(ROWS, D), w[...], preferred_element_type=F32).astype(BF16)

        def rotate(part):
            part = part.astype(F32)
            turned = part * cos_t[c] + pltpu.roll(part, HD // 2, 1) * sin_t[c]
            return turned.astype(BF16)

        qs[c] = rotate(raw[:, 0:HD])
        ks[c] = rotate(raw[:, HD:2 * HD])
        vs[c] = raw[:, 2 * HD:3 * HD]

    def attend(cq, first, count):
        index = iota((ROWS, 1), 0)
        row = CHUNK * cq + index % CHUNK
        slot = slot_of(row)
        low = slot * LMAX
        high = low + (index // CHUNK) * CAP + row - CAP * slot
        es = []
        for ck in range(first, first + count):
            kidx = iota((1, ROWS), 1)
            krow = CHUNK * ck + kidx % CHUNK
            kslot = slot_of(krow)
            within = krow - CAP * kslot
            code = kslot * LMAX + (kidx // CHUNK) * CAP + within
            code = jnp.where(within < per_slot(kslot, counts), code, RESP * LMAX)
            s = lax.dot_general(qs[cq], ks[ck], (((1,), (1,)), ((), ())), preferred_element_type=F32)
            capped = soft_cap * jnp.tanh(s * (score_scale / soft_cap))
            allowed = (code >= low) & (code <= high)
            es.append(jnp.where(allowed, jnp.exp(capped), 0.0))
        total = sum(jnp.sum(e, axis=-1, keepdims=True) for e in es)
        inverse = 1.0 / jnp.maximum(total, 1e-30)
        result = jnp.zeros((ROWS, HD), F32)
        for ck, e in zip(range(first, first + count), es):
            probs = (e * inverse).astype(BF16)
            result = result + jnp.dot(probs, vs[ck], preferred_element_type=F32)
        return result.astype(BF16).reshape(PIECES, CHUNK, HD)

    def to_pieces(k):
        send_z(lambda target: os.at[k, target], zb.at[k, core, z], p1_send.at[k], p1_recv.at[k])
        zb[k, core, z] = os[k, z]

    def share(k):
        drain(zb.at[k, core, pl.ds(0, NZ - 1)], p1_recv.at[k])
        remote(zb.at[k, core], zb.at[k, core], sib_send.at[k], sib_recv.at[k], sibling).start()

    def shared(k):
        remote(zb.at[k, 1 - core], zb.at[k, 1 - core], sib_send.at[k], sib_recv.at[k], sibling).wait_recv()

    def to_bins(h, sel):
        depth = sel.shape[-1]
        src = zb[0:depth // (NZ * 64)].reshape(depth, HD)
        rows = jnp.dot(sel[...].reshape(NZ * 32, depth), src, preferred_element_type=F32)
        ob[h] = rows.astype(BF16).reshape(NZ, 32, HD)
        place = pl.ds(pl.multiple_of(z * BIN_DEV + 32 * h, 32), 32)
        send_z(lambda target: ob.at[h, target], out.at[place], p2_send.at[h], p2_recv.at[h])
        own = pltpu.make_async_copy(ob.at[h, z], out.at[place], p2_send.at[2 + h])
        own.start()
        return own

    w_copy.wait()

    first_ring(1)
    second_ring(0)
    first_ring(2)
    second_ring(1)
    second_end(0)
    project(0)
    first_ring(3)
    second_ring(2)
    second_end(1)
    project(1)
    os[0, :, 0:CHUNK, :] = attend(0, 0, 2)
    first_ring(4)
    second_ring(3)
    second_end(2)
    project(2)
    os[0, :, CHUNK:32, :] = attend(1, 0, 3)
    to_pieces(0)
    second_ring(4)
    second_end(3)
    project(3)
    os[1, :, 0:CHUNK, :] = attend(2, 1, 3)
    os[1, :, CHUNK:32, :] = attend(3, 2, 2)
    to_pieces(1)
    share(0)
    share(1)
    shared(0)
    shared(1)
    own0 = to_bins(0, sel0)
    second_end(4)
    project(4)
    os[2, :, 0:CHUNK, :] = attend(3, 3, 2)
    os[2, :, CHUNK:32, :] = attend(4, 3, 2)
    to_pieces(2)

    reward = jnp.zeros((1, HD), F32)
    gains = readout[...].astype(F32)
    for k, (start, least, most) in enumerate(((0, 0, 32), (32, 32, 60), (48, 60, 80))):
        value = jnp.sum(os[k, PIECES - 1].astype(F32) * gains, axis=1, keepdims=True)
        row = start + iota((32, 1), 0)
        use = (row == last_row) & (row >= least) & (row < most)
        reward = reward + jnp.sum(jnp.where(use, value, 0.0), axis=0, keepdims=True)

    def sum_ring(buf, index, own, k, device_of):
        buf[index] = jnp.broadcast_to(own, (8, HD))
        for i in range(1, 4):
            remote(buf.at[index], buf.at[index], rw_send.at[k], rw_recv.at[k], device_of(i)).start()
        drain(buf.at[pl.ds(0, 3)], rw_recv.at[k])
        return (buf[0] + buf[1] + buf[2] + buf[3])[0:1, :]

    reward = sum_ring(rx, x, reward, 0, lambda i: {"tensor": y * 4 + (x + i) % 4})
    reward = sum_ring(ry, y, reward, 1, lambda i: {"tensor": ((y + i) % 4) * 4 + x})
    sc[core, z] = jnp.broadcast_to(reward - beta_weight * penalty, (8, HD))
    send_z(lambda target: sc.at[core, z], sc.at[core, z], rw_send.at[2], rw_recv.at[2])

    share(2)
    shared(2)
    own1 = to_bins(1, sel1)

    drain(sc.at[core, pl.ds(0, NZ - 1)], rw_recv.at[2])
    sc_pass = remote(sc.at[core], sc.at[core], rw_send.at[3], rw_recv.at[3], sibling)
    sc_pass.start()
    remote(sc.at[1 - core], sc.at[1 - core], rw_send.at[3], rw_recv.at[3], sibling).wait_recv()
    all_scores = sc[...].reshape(2 * NZ, 8, HD)
    sources = jnp.full((1, HD), -1, I32)
    for j in range(RESP):
        sources = jnp.where(lane == j, entry_source[0:1, j:j + 1], sources)
    mine = (tile_bin == sources.reshape(1, 1, HD)) & is_segment
    picked = jnp.sum(jnp.where(mine, all_scores, 0.0), axis=0)
    scores[...] = jnp.sum(picked, axis=0, keepdims=True)[:, 0:RESP]

    own0.wait()
    own1.wait()
    for h in range(2):
        drain(ob.at[h, pl.ds(0, NZ - 1)], p2_recv.at[h])
        drain(ob.at[h, pl.ds(0, NZ - 1)], p2_send.at[h])
    for k in range(3):
        drain(os.at[k, pl.ds(0, NZ - 1)], p1_send.at[k])
        drain(zb.at[k, core], sib_send.at[k])
    for c in range(CHUNKS):
        drain(gath.at[c, pl.ds(0, 15)], ag_send.at[c])
    drain(meta.at[core, pl.ds(0, NZ - 1)], meta_send.at[0])
    drain(meta.at[core], meta_send.at[1])
    drain(rx.at[pl.ds(0, 3)], rw_send.at[0])
    drain(ry.at[pl.ds(0, 3)], rw_send.at[1])
    drain(sc.at[core, pl.ds(0, NZ - 1)], rw_send.at[2])
    drain(sc.at[core], rw_send.at[3])


def body(responses, kl_terms, norm_gain, w_qkv, readout, slot_bin, entry_source, bin_segments):
    steps = np.arange(HD // 2, dtype=np.float32)
    frequency = (np.float32(rope_base) ** (-2.0 * steps / HD)).astype(np.float32)
    freq = jnp.asarray(np.concatenate([frequency, frequency])[None, :])
    vmem = pl.BlockSpec(memory_space=pltpu.VMEM)
    hbm = pl.BlockSpec(memory_space=pl.ANY)
    dma = pltpu.SemaphoreType.DMA
    out, scores = pl.pallas_call(
        kernel,
        out_shape=(
            jax.ShapeDtypeStruct((PIECES * BIN_DEV, HD), BF16),
            jax.ShapeDtypeStruct((1, RESP), F32),
        ),
        in_specs=[vmem, vmem, vmem, vmem, hbm, vmem, vmem, vmem, vmem],
        out_specs=(hbm, vmem),
        scratch_shapes=[
            pltpu.VMEM((CHUNKS, PIECES, CHUNK, D), BF16),
            pltpu.VMEM((D, 3 * HD), BF16),
            pltpu.VMEM((2, NZ, 8, HD), I32),
            pltpu.VMEM((CHUNKS, ROWS, HD), F32),
            pltpu.VMEM((CHUNKS, ROWS, HD), F32),
            pltpu.VMEM((CHUNKS, ROWS, HD), BF16),
            pltpu.VMEM((CHUNKS, ROWS, HD), BF16),
            pltpu.VMEM((CHUNKS, ROWS, HD), BF16),
            pltpu.VMEM((3, PIECES, 32, HD), BF16),
            pltpu.VMEM((3, 2, NZ, 32, HD), BF16),
            pltpu.VMEM((NZ, 32, 64 * NZ * 2), BF16),
            pltpu.VMEM((NZ, 32, 96 * NZ * 2), BF16),
            pltpu.VMEM((2, NZ, 32, HD), BF16),
            pltpu.VMEM((4, 8, HD), F32),
            pltpu.VMEM((4, 8, HD), F32),
            pltpu.VMEM((2, NZ, 8, HD), F32),
            dma,
            dma((CHUNKS, 4)),
            dma((CHUNKS, 4, 4)),
            dma((CHUNKS,)),
            dma((2,)),
            dma((2,)),
            dma((3,)),
            dma((3,)),
            dma((3,)),
            dma((3,)),
            dma((4,)),
            dma((2,)),
            dma((4,)),
            dma((4,)),
        ],
        compiler_params=pltpu.CompilerParams(
            collective_id=0, has_side_effects=True, vmem_limit_bytes=56 * 1024 * 1024
        ),
    )(
        responses[0], kl_terms[0], norm_gain[None, :], freq, w_qkv.reshape(D, 3 * HD),
        readout, slot_bin, entry_source, bin_segments,
    )
    return out[None], scores


def solution(mesh):
    placed = (
        P("dp", "tensor", None),
        P("dp", None, None),
        P(),
        P(None, "tensor", None),
        P("tensor", None),
        P("dp", None),
        P("dp", None),
        P("dp", None),
    )
    return jax.shard_map(
        body,
        mesh=mesh,
        in_specs=placed,
        out_specs=(P("dp", None, "tensor"), P("dp", None)),
        check_vma=False,
    )
```

time: 402 us -> 134 us (0.33); the launches traced: 395 us -> 132 us
  waiting for transfers between devices: 273 us -> 0 us
  Pallas kernels: 0 us -> 127 us
  blocking collectives: 32.1 us -> 0 us
  starting transfers between devices: 27.3 us -> 0 us
  local copies, waits for them, and re-layouts: 21.5 us -> 4.15 us
  matrix products: 14.3 us -> 0 us
  between operations: 14.2 us -> 0.64 us
  other arithmetic: 12.5 us -> 0 us
    all_to_all x2 -> x0, waiting for transfers between devices: 210 us -> none  [the longest x1 203 us: body(): lax.all_to_all(send_rows, 'dp', split_axis=0, concat_axis=0, tiled=True)]
    pallas_call x0 -> x1, Pallas kernels: none -> 127 us  [body(): pl.pallas_call(kernel, out_shape=(jax.ShapeDtypeStruct((PIECES * BIN_DEV,...]
    all_gather x1 -> x0, waiting for transfers between devices: 63.5 us -> none  [body(): lax.all_gather(normed, 'tensor', axis=0, tiled=True)]
    psum x1 -> x0, blocking collectives: 32.1 us -> none  [body(): summed = lax.psum(reward_part, 'tensor')]
    all_to_all x2 -> x0, starting transfers between devices: 27.3 us -> none  [the longest x1 15.7 us: body(): lax.all_to_all(send_rows, 'dp', split_axis=0, concat_axis=0, tiled=True)]
    dot_general x5 -> x0, matrix products: 14.3 us -> none  [the longest x1 6.55 us: body(): jnp.dot(lax.all_gather(normed, 'tensor', axis=0, tiled=True), weights, pr...]
    gather x3 -> x0, local copies, waits for them, and re-layouts: 7.44 us -> none  [the longest x1 4.49 us: body(): packed = recv_rows.reshape(groups * CAP, D)[flat_index]]
    reshape x1 -> x0, local copies, waits for them, and re-layouts: 4.89 us -> none  [body(): packed = recv_rows.reshape(groups * CAP, D)[flat_index]]
  transfers between devices with their start and end apart: 3 -> 0, of which waited for: 3 -> 0; matrix products, arithmetic and copies ran while one was open for 3% -> 0% of each run, Pallas kernels for 0% -> 0%
where the time goes in v1:
time: 134 us; the launch traced here: 132 us
  Pallas kernels  127 us (95%)
  local copies, waits for them, and re-layouts  4.15 us (3%)
    pallas_call x1, Pallas kernels, body(): pl.pallas_call(kernel, out_shape=(jax.ShapeDtypeStruct((PIECES * BIN_DEV,...  127 us
    unnamed x2, local copies, waits for them, and re-layouts  2.8 us

profile of v1, /device:TPU:6, one launch (start us, length us, event | category | flops | bytes accessed | tf_op | source)
XLA Modules:
  0.0 132.0 jit_solution(14291833934603454117)
XLA Ops:
  0.6 1.3 %broadcast_in_dim.6.gain = f32[1,4608]{1,0:T(1,128)} reshape(f32[4608]{0:T(1024)} %param.11) | data formatting | bytes 36864 | tf_op jit(solution)/shard_map/broadcast_in_dim | solution.py:439
  2.0 127.3 %shard_map.104 = (bf16[1024,128]{1,0:T(8,128)(2,1)}, f32[1,8]{1,0:T(1,128)}) custom-call(bf16[80,4608]{1,0:T(8,128)(2,1)} %bitcast.5, bf16[8,160]{1,0:T(8,128)(2,1)} %bitcast.7, f32[1,4608]{1,0:T(1,128)} %broadcast_in_dim.6.gain, f32[1,128]{1,0:T(1,128)} %constant.2.clone.freq, bf16[4608,384]{1,0:T(8,128)(2,1)} %bitcast.4, bf16[1,128]{1,0:T(2,128)(2,1)} %readout.1, ...), custom_call_target="tpu_custom_call" | custom-call | tf_op jit(solution)/shard_map/pallas_call | solution.py:395
  129.2 1.7 %copy.13 = bf16[1,1024,128]{2,1,0:T(8,128)(2,1)} copy(bf16[1,1024,128]{2,1,0:T(8,128)(2,1)} %bitcast.6) | data formatting | bytes 524288
  130.9 1.1 copy.14

commit v2 on v1

v2 whole, which is shorter than its diff:
```python
import jax
import jax.numpy as jnp
import numpy as np
from jax import lax
from jax.experimental import pallas as pl
from jax.experimental.pallas import tpu as pltpu
from jax.sharding import PartitionSpec as P

D = 4608
HD = 128
RESP = 8
CAP = 10
BIN_DEV = 64
LMAX = 160
PIECES = 16
NZ = 16
CHUNK = 16
ROWS = PIECES * CHUNK
LATE = 5
FOLD = D // 4
FOLD_LO = 640
MAIN = 256
EXTRA = 128

epsilon = 1e-06
beta_weight = 0.05
score_scale = 1.0 / 12.0
soft_cap = 50.0
rope_base = 10000.0

F32 = jnp.float32
BF16 = jnp.bfloat16
I32 = jnp.int32


def iota(shape, dim):
    return lax.broadcasted_iota(I32, shape, dim)


def slot_of(row):
    slot = jnp.zeros_like(row)
    for j in range(1, RESP):
        slot = slot + jnp.where(row >= CAP * j, 1, 0)
    return slot


def per_slot(slot, counts):
    out = jnp.zeros(slot.shape, I32)
    for j in range(RESP):
        out = jnp.where(slot == j, counts[j], out)
    return out


def kernel(
    resp, kl, gain, freq, w_hbm, readout, slot_bin, entry_source, bin_segments,
    out, scores,
    ge, gx, gl, nb, w, meta, cos_t, sin_t, low_t, high_t, code_t, qs, ks, vs,
    ib, ibx, io, iox, seli, os, zb, sel, ob, fo, rx, sc,
    w_sem, r1, r2, ag_send, meta_send, meta_recv, i_send, i_recv, ix_send, ix_recv,
    p1_send, p1_recv, sib_send, sib_recv, p2_send, p2_recv, rw_send, rw_recv, own_sem,
):
    d = lax.axis_index("dp")
    t = lax.axis_index("tensor")
    z, core = d // 2, d % 2
    y, x = t // 4, t % 4
    a = (1 - core) * x + core * y
    b = (1 - core) * y + core * x

    def piece(i, j):
        i, j = (a + i) % 4, (b + j) % 4
        return (1 - core) * (j * 4 + i) + core * (i * 4 + j)

    def in_z(target):
        return {"dp": target * 2 + core}

    sibling = {"dp": z * 2 + (1 - core)}

    def remote(src, dst, send, recv, device):
        return pltpu.make_async_remote_copy(
            src_ref=src, dst_ref=dst, send_sem=send, recv_sem=recv,
            device_id=device, device_id_type=pl.DeviceIdType.MESH,
        )

    def drain(ref, sem):
        pltpu.make_async_copy(ref, ref, sem).wait()

    def over_z(step):
        def body(i, carry):
            step((z + i) % NZ)
            return carry

        lax.fori_loop(1, NZ, body, 0)

    w_copy = pltpu.make_async_copy(w_hbm, w, w_sem)
    w_copy.start()
    barrier = pltpu.get_barrier_semaphore()

    def greet(device):
        pl.semaphore_signal(barrier, inc=1, device_id=device, device_id_type=pl.DeviceIdType.MESH)

    over_z(lambda target: greet(in_z(target)))
    for i in range(1, 4):
        greet({"tensor": piece(i, 0)})
        greet({"tensor": piece(0, i)})
    greet(sibling)

    lane = iota((1, HD), 1)
    meta[core, z] = jnp.full((8, HD), 99, I32)
    meta[core, z, 0:1, 0:BIN_DEV] = bin_segments[...]
    meta[core, z, 1:2, 0:RESP] = entry_source[...]

    gains = gain[...]
    gains = jnp.concatenate([gains[i:i + 1, :] for i in range(D // HD)], axis=1)
    for c in range(5):
        rows = resp[CHUNK * c:CHUNK * (c + 1), :].astype(F32)
        mean_square = jnp.sum(rows * rows, axis=-1, keepdims=True) * (1.0 / D)
        normed = (rows * lax.rsqrt(mean_square + epsilon) * gains).astype(BF16)
        if c < 3:
            ge[c, t] = normed
        else:
            nb[CHUNK * (c - 3):CHUNK * (c - 2), :] = normed
        if c == 3:
            wide = normed.astype(F32)
            block = iota((CHUNK, FOLD), 0) // 4
            folded = wide[:, 0:FOLD]
            for q in range(1, 4):
                part = pltpu.roll(wide[:, FOLD * q:FOLD * (q + 1)], 4 * q, 0)
                folded = jnp.where(block == q, part, folded)
            gx[t] = folded.astype(BF16)

    pl.semaphore_wait(barrier, 6 + 1 + NZ - 1)

    up_a, down_a = {"tensor": piece(1, 0)}, {"tensor": piece(-1, 0)}
    up_b, down_b = {"tensor": piece(0, 1)}, {"tensor": piece(0, -1)}
    order = (0, -1, 1, 2)

    def view(c, p, part=None):
        if c == 3:
            cut = {None: pl.ds(0, FOLD), 0: pl.ds(0, FOLD_LO), 1: pl.ds(FOLD_LO, FOLD - FOLD_LO)}[part]
            return gx.at[p, :, cut]
        cut = {None: pl.ds(0, D), 0: pl.ds(0, D // 2), 1: pl.ds(D // 2, D // 2)}[part]
        if c < 3:
            return ge.at[c, p, :, cut]
        return gl.at[p, pl.ds(CHUNK * (c - 4), CHUNK), cut]

    def full(c, p, sem, device):
        return remote(view(c, p), view(c, p), ag_send.at[c], sem, device)

    def half(c, p, part, sem, device):
        return remote(view(c, p, part), view(c, p, part), ag_send.at[c], sem, device)

    def second_sends(c, i):
        p = piece(order[i], 0)
        full(c, p, r2.at[c, i, 0], up_b).start()
        full(c, p, r2.at[c, i, 1], down_b).start()

    def first_sends(c):
        full(c, t, r1.at[c, 0], up_a).start()
        full(c, t, r1.at[c, 1], down_a).start()

    def first_ring(c):
        full(c, piece(-1, 0), r1.at[c, 0], up_a).wait_recv()
        half(c, piece(-1, 0), 0, r1.at[c, 2], up_a).start()
        second_sends(c, 1)
        full(c, piece(1, 0), r1.at[c, 1], down_a).wait_recv()
        half(c, piece(1, 0), 1, r1.at[c, 3], down_a).start()
        second_sends(c, 2)
        half(c, piece(2, 0), 0, r1.at[c, 2], up_a).wait_recv()
        half(c, piece(2, 0), 1, r1.at[c, 3], down_a).wait_recv()
        second_sends(c, 3)

    def second_ring(c):
        for i in range(4):
            below, above = piece(order[i], -1), piece(order[i], 1)
            full(c, below, r2.at[c, i, 0], up_b).wait_recv()
            half(c, below, 0, r2.at[c, i, 2], up_b).start()
            full(c, above, r2.at[c, i, 1], down_b).wait_recv()
            half(c, above, 1, r2.at[c, i, 3], down_b).start()

    def second_end(c):
        for i in range(4):
            opposite = piece(order[i], 2)
            half(c, opposite, 0, r2.at[c, i, 2], up_b).wait_recv()
            half(c, opposite, 1, r2.at[c, i, 3], down_b).wait_recv()

    def main_cols(target):
        return pl.ds(pl.multiple_of(target * MAIN, MAIN), MAIN)

    def extra_cols(target):
        return pl.ds(pl.multiple_of(NZ * MAIN + (target // 4) * EXTRA, EXTRA), EXTRA)

    def spread(target):
        remote(nb.at[:, main_cols(target)], ib.at[core, z], i_send.at[0], i_recv.at[0], in_z(target)).start()

        @pl.when(target % 4 == 0)
        def _():
            remote(nb.at[:, extra_cols(target)], ibx.at[core, z], ix_send.at[0], ix_recv.at[0], in_z(target)).start()

    def collect(target):
        remote(io.at[target], gl.at[t, :, main_cols(z)], i_send.at[1], i_recv.at[1], in_z(target)).start()

        @pl.when(z % 4 == 0)
        def _():
            remote(iox.at[target], gl.at[t, :, extra_cols(z)], ix_send.at[1], ix_recv.at[1], in_z(target)).start()

    first_sends(0)
    second_sends(0, 0)
    first_sends(1)
    over_z(spread)
    first_sends(2)
    first_sends(3)
    over_z(lambda target: remote(
        meta.at[core, z], meta.at[core, z], meta_send.at[0], meta_recv.at[0], in_z(target)).start())
    ib[core, z] = nb[:, main_cols(z)]

    @pl.when(z % 4 == 0)
    def _():
        ibx[core, z] = nb[:, extra_cols(z)]

    first_ring(0)
    second_sends(1, 0)
    first_ring(1)

    drain(meta.at[core, pl.ds(0, NZ - 1)], meta_recv.at[0])
    meta_pass = remote(meta.at[core], meta.at[core], meta_send.at[1], meta_recv.at[1], sibling)
    meta_pass.start()
    second_ring(0)

    def bin_rows(tile, start, size):
        seg_row = tile[0:1, :].astype(F32)
        src_row = tile[1:2, :].astype(F32)
        r_col = start + iota((size, HD), 0)
        l_row = iota((size, HD), 1)
        seg = jnp.sum(jnp.where(r_col == l_row, seg_row, 0.0), axis=1, keepdims=True)
        number = jnp.sum(jnp.where(seg_row == seg, 1.0, 0.0), axis=1, keepdims=True)
        offset = jnp.sum(jnp.where(seg_row < seg, 1.0, 0.0), axis=1, keepdims=True)
        source = jnp.sum(jnp.where(l_row.astype(F32) == seg, src_row, 0.0), axis=1, keepdims=True)
        source = source.astype(I32)
        within = r_col[:, 0:1].astype(F32) - offset
        return seg, number, within, (source & 1) * NZ + (source >> 1)

    def pick_late(i, carry):
        seg, _, within, place = bin_rows(meta[core, i], 32, 32)
        row = CAP * seg.astype(I32) + within.astype(I32) - 48
        column = jnp.where(seg >= LATE, place * 32 + row, -1)
        seli[i] = jnp.where(iota((32, 2 * NZ * 32), 1) == column, 1.0, 0.0).astype(BF16)
        return carry

    lax.fori_loop(0, NZ, pick_late, 0)

    drain(ib.at[core, pl.ds(0, NZ - 1)], i_recv.at[0])
    ib_pass = remote(ib.at[core], ib.at[core], sib_send.at[2], sib_recv.at[2], sibling)
    ib_pass.start()

    @pl.when(z % 4 == 0)
    def _():
        drain(ibx.at[core, pl.ds(0, NZ - 1)], ix_recv.at[0])
        remote(ibx.at[core], ibx.at[core], sib_send.at[3], sib_recv.at[3], sibling).start()

    second_sends(2, 0)
    first_ring(2)
    second_ring(1)

    remote(ib.at[1 - core], ib.at[1 - core], sib_send.at[2], sib_recv.at[2], sibling).wait_recv()
    picks = seli[...].reshape(NZ * 32, 2 * NZ * 32)
    rows = jnp.dot(picks, ib[...].reshape(2 * NZ * 32, MAIN), preferred_element_type=F32)
    io[...] = rows.astype(BF16).reshape(NZ, 32, MAIN)

    @pl.when(z % 4 == 0)
    def _():
        remote(ibx.at[1 - core], ibx.at[1 - core], sib_send.at[3], sib_recv.at[3], sibling).wait_recv()
        rows = jnp.dot(picks, ibx[...].reshape(2 * NZ * 32, EXTRA), preferred_element_type=F32)
        iox[...] = rows.astype(BF16).reshape(NZ, 32, EXTRA)

    over_z(collect)
    gl[t, :, main_cols(z)] = io[z]

    @pl.when(z % 4 == 0)
    def _():
        gl[t, :, extra_cols(z)] = iox[z]

    remote(meta.at[1 - core], meta.at[1 - core], meta_send.at[1], meta_recv.at[1], sibling).wait_recv()

    every = meta[...].reshape(2 * NZ, 8, HD)
    tile_row = iota((2 * NZ, 8, HD), 1)
    tile_id = iota((2 * NZ, 8, HD), 0)
    tile_bin = (tile_id % NZ) * 2 + tile_id // NZ
    is_segment = tile_row == 0
    counts = []
    for j in range(RESP):
        hit = is_segment & (every == j) & (tile_bin == slot_bin[0:1, j:j + 1].reshape(1, 1, 1))
        counts.append(jnp.sum(jnp.where(hit, 1.0, 0.0)).astype(I32))

    def rope_tables(c, carry):
        index = iota((ROWS, HD), 0)
        row = CHUNK * c + index % CHUNK
        slot = slot_of(row)
        position = (index // CHUNK) * per_slot(slot, counts) + row - CAP * slot
        angle = position.astype(F32) * freq[...]
        cos_t[c] = jnp.cos(angle)
        sine = jnp.sin(angle)
        sin_t[c] = jnp.where(iota((ROWS, HD), 1) < HD // 2, -sine, sine)
        return carry

    def rotated(raw, c):
        def rotate(part):
            part = part.astype(F32)
            turned = part * cos_t[c] + pltpu.roll(part, HD // 2, 1) * sin_t[c]
            return turned.astype(BF16)

        qs[c] = rotate(raw[:, 0:HD])
        ks[c] = rotate(raw[:, HD:2 * HD])
        vs[c] = raw[:, 2 * HD:3 * HD]

    def project(c):
        rows = ge[c] if c < 3 else gl[:, CHUNK * (c - 4):CHUNK * (c - 3), :]
        raw = jnp.dot(rows.reshape(ROWS, D), w[...], preferred_element_type=F32)
        rotated(raw.astype(BF16), c)

    def project_folded():
        rows = gx[...].reshape(ROWS, FOLD)
        raw = jnp.dot(rows, w[0:FOLD, :], preferred_element_type=F32)
        for q in range(1, 4):
            part = jnp.dot(rows, w[FOLD * q:FOLD * (q + 1), :], preferred_element_type=F32)
            raw = raw + pltpu.roll(part, ROWS - 4 * q, 0)
        rotated(raw.astype(BF16), 3)

    def softmax_values(q, low, high, keys):
        es = []
        for ck, code in keys:
            s = lax.dot_general(q, ks[ck], (((1,), (1,)), ((), ())), preferred_element_type=F32)
            capped = soft_cap * jnp.tanh(s * (score_scale / soft_cap))
            allowed = (code >= low) & (code <= high)
            es.append(jnp.where(allowed, jnp.exp(capped), 0.0))
        total = sum(jnp.sum(e, axis=-1, keepdims=True) for e in es)
        inverse = 1.0 / jnp.maximum(total, 1e-30)
        result = jnp.zeros((q.shape[0], HD), F32)
        for (ck, _), e in zip(keys, es):
            result = result + jnp.dot((e * inverse).astype(BF16), vs[ck], preferred_element_type=F32)
        return result.astype(BF16)

    def attend(cq, first, count):
        index = iota((ROWS, 1), 0)
        row = CHUNK * cq + index % CHUNK
        slot = slot_of(row)
        low = slot * LMAX
        high = low + (index // CHUNK) * CAP + row - CAP * slot
        keys = []
        for ck in range(first, first + count):
            kidx = iota((1, ROWS), 1)
            krow = CHUNK * ck + kidx % CHUNK
            kslot = slot_of(krow)
            within = krow - CAP * kslot
            code = kslot * LMAX + (kidx // CHUNK) * CAP + within
            live = (within < per_slot(kslot, counts)) & (kslot < LATE)
            keys.append((ck, jnp.where(live, code, 2 * RESP * LMAX)))
        return softmax_values(qs[cq], low, high, keys).reshape(PIECES, CHUNK, HD)

    def to_pieces(k):
        over_z(lambda target: remote(
            os.at[k, target], zb.at[k, core, z], p1_send.at[k], p1_recv.at[k], in_z(target)).start())
        zb[k, core, z] = os[k, z]

    def share(k):
        drain(zb.at[k, core, pl.ds(0, NZ - 1)], p1_recv.at[k])
        remote(zb.at[k, core], zb.at[k, core], sib_send.at[k], sib_recv.at[k], sibling).start()

    def shared(k):
        remote(zb.at[k, 1 - core], zb.at[k, 1 - core], sib_send.at[k], sib_recv.at[k], sibling).wait_recv()

    def pick_early(i, carry):
        seg, _, within, place = bin_rows(meta[core, i], 0, BIN_DEV)
        row = CAP * seg.astype(I32) + within.astype(I32)
        column = place * 32 + jnp.where(row < 32, row, 2 * NZ * 32 + row - 32)
        column = jnp.where(seg < LATE, column, -1)
        sel[i] = jnp.where(iota((BIN_DEV, 2 * NZ * 64), 1) == column, 1.0, 0.0).astype(BF16)
        return carry

    def late_tables():
        seg, number, within, _ = bin_rows(meta[core, z], 32, 32)
        for c in range(2):
            def spread_rows(col):
                col = col[CHUNK * c:CHUNK * (c + 1)].reshape(1, CHUNK, 1)
                return jnp.broadcast_to(col, (PIECES, CHUNK, HD)).reshape(ROWS, HD)

            slot = spread_rows(seg)
            position = (iota((ROWS, HD), 0) // CHUNK).astype(F32) * spread_rows(number) + spread_rows(within)
            angle = position * freq[...]
            cos_t[4 + c] = jnp.cos(angle)
            sine = jnp.sin(angle)
            sin_t[4 + c] = jnp.where(iota((ROWS, HD), 1) < HD // 2, -sine, sine)
            live = slot >= LATE
            low_t[c] = jnp.where(live, slot * LMAX, 4.0 * RESP * LMAX)
            high_t[c] = jnp.where(live, slot * LMAX + position, -1.0)
            code = jnp.where(live, slot * LMAX + position, 2.0 * RESP * LMAX)
            code_t[c] = jnp.transpose(code)[0:8, :]

    def late_keys():
        return [(4, code_t[0, 0:1, :]), (5, code_t[1, 0:1, :])]

    lax.fori_loop(0, 4, rope_tables, 0)
    w_copy.wait()
    second_end(0)
    project(0)
    first_ring(3)
    second_sends(3, 0)
    second_ring(2)
    second_end(1)
    project(1)
    os[0, :, 0:CHUNK, :] = attend(0, 0, 2)
    second_ring(3)
    lax.fori_loop(0, NZ, pick_early, 0)
    second_end(3)
    project_folded()
    second_end(2)
    project(2)
    os[1, :, 0:CHUNK, :] = attend(2, 1, 3)
    os[1, :, CHUNK:32, :] = attend(3, 2, 2)
    to_pieces(1)

    drain(io.at[pl.ds(0, NZ - 1)], i_recv.at[1])

    @pl.when(z % 4 == 0)
    def _():
        drain(iox.at[pl.ds(0, 3)], ix_recv.at[1])

    @pl.when(z % 4 != 0)
    def _():
        drain(iox.at[pl.ds(0, 4)], ix_recv.at[1])

    first_sends(4)
    second_sends(4, 0)
    first_sends(5)
    os[0, :, CHUNK:32, :] = attend(1, 0, 3)
    to_pieces(0)
    first_ring(4)

    weights = readout[...].astype(F32)
    last_row = jnp.full((1, HD), -1, I32)
    penalty = jnp.zeros((1, HD), F32)
    token = iota((1, LMAX), 1)
    for j in range(RESP):
        if j < LATE:
            last_row = jnp.where(lane == j, CAP * j + counts[j] - 1, last_row)
        live = jnp.where(token < counts[j] * PIECES, kl[j:j + 1, :].astype(F32), 0.0)
        penalty = jnp.where(lane == j, jnp.sum(live, axis=1, keepdims=True), penalty)

    def reward_of(rows, row, wanted):
        value = jnp.sum(rows.astype(F32) * weights, axis=1, keepdims=True)
        return jnp.sum(jnp.where(row == wanted, value, 0.0), axis=0, keepdims=True)

    reward = jnp.zeros((1, HD), F32)
    for k in range(2):
        reward = reward + reward_of(os[k, PIECES - 1], 32 * k + iota((32, 1), 0), last_row)

    def ring_x(i):
        return {"tensor": y * 4 + (x + i) % 4}

    def ring_y(i):
        return {"tensor": ((y + i) % 4) * 4 + x}

    def sum_start(buf, k, index, own, device_of):
        buf[k, index] = jnp.broadcast_to(own, (8, HD))
        for i in range(1, 4):
            remote(buf.at[k, index], buf.at[k, index], rw_send.at[k], rw_recv.at[k], device_of(i)).start()

    def sum_end(buf, k):
        drain(buf.at[k, pl.ds(0, 3)], rw_recv.at[k])
        return (buf[k, 0] + buf[k, 1] + buf[k, 2] + buf[k, 3])[0:1, :]

    sum_start(rx, 0, x, reward, ring_x)
    late_tables()
    second_ring(4)
    second_sends(5, 0)
    first_ring(5)
    reward = sum_end(rx, 0)
    sum_start(rx, 1, y, reward, ring_y)
    share(1)
    share(0)
    reward = sum_end(rx, 1)
    sc[core, z] = jnp.broadcast_to(reward - beta_weight * penalty, (8, HD))
    over_z(lambda target: remote(
        sc.at[core, z], sc.at[core, z], rw_send.at[4], rw_recv.at[4], in_z(target)).start())
    shared(1)
    shared(0)
    src = zb[...].reshape(2 * NZ * 64, HD)
    rows = jnp.dot(sel[...].reshape(NZ * BIN_DEV, 2 * NZ * 64), src, preferred_element_type=F32)
    ob[...] = rows.astype(BF16).reshape(NZ, BIN_DEV, HD)
    over_z(lambda target: remote(
        ob.at[target], fo.at[z], p2_send, p2_recv, in_z(target)).start())
    fo[z] = ob[z]

    second_ring(5)
    second_end(4)
    project(4)
    drain(sc.at[core, pl.ds(0, NZ - 1)], rw_recv.at[4])
    sc_pass = remote(sc.at[core], sc.at[core], rw_send.at[5], rw_recv.at[5], sibling)
    sc_pass.start()

    seg_row = meta[core, z, 0:1, :]
    late_last = jnp.full((1, HD), -1, I32)
    for j in range(LATE, RESP):
        upto = jnp.sum(jnp.where(seg_row <= j, 1.0, 0.0), axis=1, keepdims=True).astype(I32)
        late_last = jnp.where(lane == j, upto - 33, late_last)

    second_end(5)
    project(5)
    tail = pl.ds(ROWS - CHUNK, CHUNK)
    q_last = jnp.concatenate([qs[4, tail, :], qs[5, tail, :]], axis=0)
    low = jnp.concatenate([low_t[0, tail, 0:1], low_t[1, tail, 0:1]], axis=0)
    high = jnp.concatenate([high_t[0, tail, 0:1], high_t[1, tail, 0:1]], axis=0)
    last_rows = softmax_values(q_last, low, high, late_keys())
    sum_start(rx, 2, x, reward_of(last_rows, iota((32, 1), 0), late_last), ring_x)
    late = []
    late.append(softmax_values(qs[4], low_t[0, :, 0:1], high_t[0, :, 0:1], late_keys()))
    reward = sum_end(rx, 2)
    sum_start(rx, 3, y, reward, ring_y)
    late.append(softmax_values(qs[5], low_t[1, :, 0:1], high_t[1, :, 0:1], late_keys()))

    drain(ob.at[pl.ds(0, NZ - 1)], p2_recv)
    for c in range(2):
        rows = pl.ds(32 + CHUNK * c, CHUNK)
        mine = late[c].reshape(PIECES, CHUNK, HD).astype(F32)
        fo[:, rows, :] = (fo[:, rows, :].astype(F32) + mine).astype(BF16)
    out_copy = pltpu.make_async_copy(fo, out, own_sem)
    out_copy.start()

    remote(sc.at[1 - core], sc.at[1 - core], rw_send.at[5], rw_recv.at[5], sibling).wait_recv()
    all_scores = sc[...].reshape(2 * NZ, 8, HD)
    sources = jnp.full((1, HD), -1, I32)
    for j in range(RESP):
        sources = jnp.where(lane == j, entry_source[0:1, j:j + 1], sources)
    mine = (tile_bin == sources.reshape(1, 1, HD)) & is_segment
    picked = jnp.sum(jnp.where(mine, all_scores, 0.0), axis=0)
    picked = jnp.sum(picked, axis=0, keepdims=True)

    for c in range(6):
        if c < 3:
            sent = ge.at[c, pl.ds(0, 15)]
        elif c == 3:
            sent = gx.at[pl.ds(0, 15)]
        else:
            sent = gl.at[pl.ds(0, 15), pl.ds(CHUNK * (c - 4), CHUNK)]
        drain(sent, ag_send.at[c])
    drain(io.at[pl.ds(0, NZ - 1)], i_send.at[0])
    drain(io.at[pl.ds(0, NZ - 1)], i_send.at[1])

    @pl.when(z % 4 == 0)
    def _():
        drain(iox.at[pl.ds(0, 3)], ix_send.at[0])
        drain(iox.at[pl.ds(0, NZ - 1)], ix_send.at[1])
        drain(ibx.at[core], sib_send.at[3])

    @pl.when(z % 4 != 0)
    def _():
        drain(iox.at[pl.ds(0, 4)], ix_send.at[0])

    for k in range(2):
        drain(os.at[k, pl.ds(0, NZ - 1)], p1_send.at[k])
        drain(zb.at[k, core], sib_send.at[k])
    drain(ib.at[core], sib_send.at[2])
    drain(ob.at[pl.ds(0, NZ - 1)], p2_send)
    drain(meta.at[core, pl.ds(0, NZ - 1)], meta_send.at[0])
    drain(meta.at[core], meta_send.at[1])
    for k in range(3):
        drain(rx.at[k, pl.ds(0, 3)], rw_send.at[k])
    drain(sc.at[core, pl.ds(0, NZ - 1)], rw_send.at[4])
    drain(sc.at[core], rw_send.at[5])
    reward = sum_end(rx, 3)
    scores[...] = (picked + reward)[:, 0:RESP]
    drain(rx.at[3, pl.ds(0, 3)], rw_send.at[3])
    out_copy.wait()


def body(responses, kl_terms, norm_gain, w_qkv, readout, slot_bin, entry_source, bin_segments):
    steps = np.arange(HD // 2, dtype=np.float32)
    frequency = (np.float32(rope_base) ** (-2.0 * steps / HD)).astype(np.float32)
    freq = jnp.asarray(np.concatenate([frequency, frequency])[None, :])
    vmem = pl.BlockSpec(memory_space=pltpu.VMEM)
    hbm = pl.BlockSpec(memory_space=pl.ANY)
    dma = pltpu.SemaphoreType.DMA
    out, scores = pl.pallas_call(
        kernel,
        out_shape=(
            jax.ShapeDtypeStruct((PIECES, BIN_DEV, HD), BF16),
            jax.ShapeDtypeStruct((1, RESP), F32),
        ),
        in_specs=[vmem, vmem, vmem, vmem, hbm, vmem, vmem, vmem, vmem],
        out_specs=(hbm, vmem),
        scratch_shapes=[
            pltpu.VMEM((3, PIECES, CHUNK, D), BF16),
            pltpu.VMEM((PIECES, CHUNK, FOLD), BF16),
            pltpu.VMEM((PIECES, 2 * CHUNK, D), BF16),
            pltpu.VMEM((2 * CHUNK, D), BF16),
            pltpu.VMEM((D, 3 * HD), BF16),
            pltpu.VMEM((2, NZ, 8, HD), I32),
            pltpu.VMEM((6, ROWS, HD), F32),
            pltpu.VMEM((6, ROWS, HD), F32),
            pltpu.VMEM((2, ROWS, HD), F32),
            pltpu.VMEM((2, ROWS, HD), F32),
            pltpu.VMEM((2, 8, ROWS), F32),
            pltpu.VMEM((6, ROWS, HD), BF16),
            pltpu.VMEM((6, ROWS, HD), BF16),
            pltpu.VMEM((6, ROWS, HD), BF16),
            pltpu.VMEM((2, NZ, 32, MAIN), BF16),
            pltpu.VMEM((2, NZ, 32, EXTRA), BF16),
            pltpu.VMEM((NZ, 32, MAIN), BF16),
            pltpu.VMEM((NZ, 32, EXTRA), BF16),
            pltpu.VMEM((NZ, 32, 2 * NZ * 32), BF16),
            pltpu.VMEM((2, PIECES, 32, HD), BF16),
            pltpu.VMEM((2, 2, NZ, 32, HD), BF16),
            pltpu.VMEM((NZ, BIN_DEV, 2 * NZ * 64), BF16),
            pltpu.VMEM((NZ, BIN_DEV, HD), BF16),
            pltpu.VMEM((PIECES, BIN_DEV, HD), BF16),
            pltpu.VMEM((4, 4, 8, HD), F32),
            pltpu.VMEM((2, NZ, 8, HD), F32),
            dma,
            dma((6, 4)),
            dma((6, 4, 4)),
            dma((6,)),
            dma((2,)),
            dma((2,)),
            dma((2,)),
            dma((2,)),
            dma((2,)),
            dma((2,)),
            dma((2,)),
            dma((2,)),
            dma((4,)),
            dma((4,)),
            dma,
            dma,
            dma((6,)),
            dma((6,)),
            dma,
        ],
        compiler_params=pltpu.CompilerParams(
            collective_id=0, has_side_effects=True, vmem_limit_bytes=58 * 1024 * 1024
        ),
    )(
        responses[0], kl_terms[0], norm_gain.reshape(D // HD, HD), freq, w_qkv.reshape(D, 3 * HD),
        readout, slot_bin, entry_source, bin_segments,
    )
    return out.reshape(1, PIECES * BIN_DEV, HD), scores


def solution(mesh):
    placed = (
        P("dp", "tensor", None),
        P("dp", None, None),
        P(),
        P(None, "tensor", None),
        P("tensor", None),
        P("dp", None),
        P("dp", None),
        P("dp", None),
    )
    return jax.shard_map(
        body,
        mesh=mesh,
        in_specs=placed,
        out_specs=(P("dp", None, "tensor"), P("dp", None)),
        check_vma=False,
    )
```

time: 134 us -> 116 us (0.87)
  Pallas kernels: 127 us -> 111 us
  local copies, waits for them, and re-layouts: 4.15 us -> 2.8 us
    pallas_call x1, Pallas kernels: 127 us -> 111 us  [body(): pl.pallas_call(kernel, out_shape=(jax.ShapeDtypeStruct((PIECES, BIN_DEV,...]
    broadcast_in_dim x1 -> x0, local copies, waits for them, and re-layouts: 1.35 us -> none  [body(): norm_gain[None, :]]
where the time goes in v2:
time: 116 us; the launch traced here: 115 us
  Pallas kernels  111 us (96%)
  local copies, waits for them, and re-layouts  2.8 us (2%)
    pallas_call x1, Pallas kernels, body(): pl.pallas_call(kernel, out_shape=(jax.ShapeDtypeStruct((PIECES, BIN_DEV,...  111 us
    unnamed x2, local copies, waits for them, and re-layouts  2.8 us

profile of v2, /device:TPU:6, one launch (start us, length us, event | category | flops | bytes accessed | tf_op | source)
XLA Modules:
  0.0 114.8 jit_solution(14730661669480237314)
XLA Ops:
  0.6 111.4 %shard_map.104 = (bf16[16,64,128]{2,1,0:T(8,128)(2,1)}, f32[1,8]{1,0:T(1,128)}) custom-call(bf16[80,4608]{1,0:T(8,128)(2,1)} %bitcast.6, bf16[8,160]{1,0:T(8,128)(2,1)} %bitcast.9, f32[36,128]{1,0:T(8,128)} %bitcast.8, f32[1,128]{1,0:T(1,128)} %constant.2.clone.freq, bf16[4608,384]{1,0:T(8,128)(2,1)} %bitcast.5, bf16[1,128]{1,0:T(2,128)(2,1)} %readout.1, ...), custom_call_target="tpu_custom_call" | custom-call | tf_op jit(solution)/shard_map/pallas_call | solution.py:582
  112.0 1.7 %copy.13 = bf16[1,1024,128]{2,1,0:T(8,128)(2,1)} copy(bf16[1,1024,128]{2,1,0:T(8,128)(2,1)} %bitcast.7) | data formatting | bytes 524288
  113.7 1.1 copy.14

commit v3 on v2

--- a/solution.py
+++ b/solution.py
@@ -91,6 +91,13 @@
 
         lax.fori_loop(1, NZ, body, 0)
 
+    def over_plane(step):
+        def body(i, carry):
+            step((t + i) % PIECES)
+            return carry
+
+        lax.fori_loop(1, PIECES, body, 0)
+
     w_copy = pltpu.make_async_copy(w_hbm, w, w_sem)
     w_copy.start()
     barrier = pltpu.get_barrier_semaphore()
@@ -99,9 +106,7 @@
         pl.semaphore_signal(barrier, inc=1, device_id=device, device_id_type=pl.DeviceIdType.MESH)
 
     over_z(lambda target: greet(in_z(target)))
-    for i in range(1, 4):
-        greet({"tensor": piece(i, 0)})
-        greet({"tensor": piece(0, i)})
+    over_plane(lambda target: greet({"tensor": target}))
     greet(sibling)
 
     lane = iota((1, HD), 1)
@@ -128,7 +133,7 @@
                 folded = jnp.where(block == q, part, folded)
             gx[t] = folded.astype(BF16)
 
-    pl.semaphore_wait(barrier, 6 + 1 + NZ - 1)
+    pl.semaphore_wait(barrier, PIECES - 1 + 1 + NZ - 1)
 
     up_a, down_a = {"tensor": piece(1, 0)}, {"tensor": piece(-1, 0)}
     up_b, down_b = {"tensor": piece(0, 1)}, {"tensor": piece(0, -1)}
@@ -203,28 +208,31 @@
         def _():
             remote(iox.at[target], gl.at[t, :, extra_cols(z)], ix_send.at[1], ix_recv.at[1], in_z(target)).start()
 
+    first_sends(3)
+    second_sends(3, 0)
     first_sends(0)
     second_sends(0, 0)
+    over_z(spread)
     first_sends(1)
-    over_z(spread)
-    first_sends(2)
-    first_sends(3)
+    second_sends(1, 0)
     over_z(lambda target: remote(
         meta.at[core, z], meta.at[core, z], meta_send.at[0], meta_recv.at[0], in_z(target)).start())
+    first_sends(2)
     ib[core, z] = nb[:, main_cols(z)]
 
     @pl.when(z % 4 == 0)
     def _():
         ibx[core, z] = nb[:, extra_cols(z)]
 
+    first_ring(3)
     first_ring(0)
-    second_sends(1, 0)
+    second_sends(2, 0)
+    second_ring(3)
     first_ring(1)
 
     drain(meta.at[core, pl.ds(0, NZ - 1)], meta_recv.at[0])
     meta_pass = remote(meta.at[core], meta.at[core], meta_send.at[1], meta_recv.at[1], sibling)
     meta_pass.start()
-    second_ring(0)
 
     def bin_rows(tile, start, size):
         seg_row = tile[0:1, :].astype(F32)
@@ -246,8 +254,35 @@
         seli[i] = jnp.where(iota((32, 2 * NZ * 32), 1) == column, 1.0, 0.0).astype(BF16)
         return carry
 
+    def late_tables():
+        seg, number, within, _ = bin_rows(meta[core, z], 32, 32)
+        for c in range(2):
+            def spread_rows(col):
+                col = col[CHUNK * c:CHUNK * (c + 1)].reshape(1, CHUNK, 1)
+                return jnp.broadcast_to(col, (PIECES, CHUNK, HD)).reshape(ROWS, HD)
+
+            slot = spread_rows(seg)
+            position = (iota((ROWS, HD), 0) // CHUNK).astype(F32) * spread_rows(number) + spread_rows(within)
+            angle = position * freq[...]
+            cos_t[4 + c] = jnp.cos(angle)
+            sine = jnp.sin(angle)
+            sin_t[4 + c] = jnp.where(iota((ROWS, HD), 1) < HD // 2, -sine, sine)
+            live = slot >= LATE
+            low_t[c] = jnp.where(live, slot * LMAX, 4.0 * RESP * LMAX)
+            high_t[c] = jnp.where(live, slot * LMAX + position, -1.0)
+            code = jnp.where(live, slot * LMAX + position, 2.0 * RESP * LMAX)
+            code_t[c] = jnp.transpose(code)[0:8, :]
+
+    late_tables()
+    def pick_early(i, carry):
+        seg, _, within, place = bin_rows(meta[core, i], 0, BIN_DEV)
+        row = CAP * seg.astype(I32) + within.astype(I32)
+        column = place * 32 + jnp.where(row < 30, row, 2 * NZ * 32 + jnp.where(row < 32, row, row - 32))
+        column = jnp.where(seg < LATE, column, -1)
+        sel[i] = jnp.where(iota((BIN_DEV, 2 * NZ * 64), 1) == column, 1.0, 0.0).astype(BF16)
+        return carry
+
     lax.fori_loop(0, NZ, pick_late, 0)
-
     drain(ib.at[core, pl.ds(0, NZ - 1)], i_recv.at[0])
     ib_pass = remote(ib.at[core], ib.at[core], sib_send.at[2], sib_recv.at[2], sibling)
     ib_pass.start()
@@ -257,10 +292,7 @@
         drain(ibx.at[core, pl.ds(0, NZ - 1)], ix_recv.at[0])
         remote(ibx.at[core], ibx.at[core], sib_send.at[3], sib_recv.at[3], sibling).start()
 
-    second_sends(2, 0)
-    first_ring(2)
-    second_ring(1)
-
+    second_ring(0)
     remote(ib.at[1 - core], ib.at[1 - core], sib_send.at[2], sib_recv.at[2], sibling).wait_recv()
     picks = seli[...].reshape(NZ * 32, 2 * NZ * 32)
     rows = jnp.dot(picks, ib[...].reshape(2 * NZ * 32, MAIN), preferred_element_type=F32)
@@ -279,28 +311,9 @@
     def _():
         gl[t, :, extra_cols(z)] = iox[z]
 
-    remote(meta.at[1 - core], meta.at[1 - core], meta_send.at[1], meta_recv.at[1], sibling).wait_recv()
-
-    every = meta[...].reshape(2 * NZ, 8, HD)
-    tile_row = iota((2 * NZ, 8, HD), 1)
-    tile_id = iota((2 * NZ, 8, HD), 0)
-    tile_bin = (tile_id % NZ) * 2 + tile_id // NZ
-    is_segment = tile_row == 0
-    counts = []
-    for j in range(RESP):
-        hit = is_segment & (every == j) & (tile_bin == slot_bin[0:1, j:j + 1].reshape(1, 1, 1))
-        counts.append(jnp.sum(jnp.where(hit, 1.0, 0.0)).astype(I32))
-
-    def rope_tables(c, carry):
-        index = iota((ROWS, HD), 0)
-        row = CHUNK * c + index % CHUNK
-        slot = slot_of(row)
-        position = (index // CHUNK) * per_slot(slot, counts) + row - CAP * slot
-        angle = position.astype(F32) * freq[...]
-        cos_t[c] = jnp.cos(angle)
-        sine = jnp.sin(angle)
-        sin_t[c] = jnp.where(iota((ROWS, HD), 1) < HD // 2, -sine, sine)
-        return carry
+    second_end(3)
+    first_ring(2)
+    second_ring(1)
 
     def rotated(raw, c):
         def rotate(part):
@@ -368,72 +381,69 @@
     def shared(k):
         remote(zb.at[k, 1 - core], zb.at[k, 1 - core], sib_send.at[k], sib_recv.at[k], sibling).wait_recv()
 
-    def pick_early(i, carry):
-        seg, _, within, place = bin_rows(meta[core, i], 0, BIN_DEV)
-        row = CAP * seg.astype(I32) + within.astype(I32)
-        column = place * 32 + jnp.where(row < 32, row, 2 * NZ * 32 + row - 32)
-        column = jnp.where(seg < LATE, column, -1)
-        sel[i] = jnp.where(iota((BIN_DEV, 2 * NZ * 64), 1) == column, 1.0, 0.0).astype(BF16)
-        return carry
-
-    def late_tables():
-        seg, number, within, _ = bin_rows(meta[core, z], 32, 32)
-        for c in range(2):
-            def spread_rows(col):
-                col = col[CHUNK * c:CHUNK * (c + 1)].reshape(1, CHUNK, 1)
-                return jnp.broadcast_to(col, (PIECES, CHUNK, HD)).reshape(ROWS, HD)
-
-            slot = spread_rows(seg)
-            position = (iota((ROWS, HD), 0) // CHUNK).astype(F32) * spread_rows(number) + spread_rows(within)
-            angle = position * freq[...]
-            cos_t[4 + c] = jnp.cos(angle)
-            sine = jnp.sin(angle)
-            sin_t[4 + c] = jnp.where(iota((ROWS, HD), 1) < HD // 2, -sine, sine)
-            live = slot >= LATE
-            low_t[c] = jnp.where(live, slot * LMAX, 4.0 * RESP * LMAX)
-            high_t[c] = jnp.where(live, slot * LMAX + position, -1.0)
-            code = jnp.where(live, slot * LMAX + position, 2.0 * RESP * LMAX)
-            code_t[c] = jnp.transpose(code)[0:8, :]
-
     def late_keys():
         return [(4, code_t[0, 0:1, :]), (5, code_t[1, 0:1, :])]
 
+    remote(meta.at[1 - core], meta.at[1 - core], meta_send.at[1], meta_recv.at[1], sibling).wait_recv()
+
+    every = meta[...].reshape(2 * NZ, 8, HD)
+    tile_row = iota((2 * NZ, 8, HD), 1)
+    tile_id = iota((2 * NZ, 8, HD), 0)
+    tile_bin = (tile_id % NZ) * 2 + tile_id // NZ
+    is_segment = tile_row == 0
+    counts = []
+    for j in range(RESP):
+        hit = is_segment & (every == j) & (tile_bin == slot_bin[0:1, j:j + 1].reshape(1, 1, 1))
+        counts.append(jnp.sum(jnp.where(hit, 1.0, 0.0)).astype(I32))
+
+    def rope_tables(c, carry):
+        index = iota((ROWS, HD), 0)
+        row = CHUNK * c + index % CHUNK
+        slot = slot_of(row)
+        position = (index // CHUNK) * per_slot(slot, counts) + row - CAP * slot
+        angle = position.astype(F32) * freq[...]
+        cos_t[c] = jnp.cos(angle)
+        sine = jnp.sin(angle)
+        sin_t[c] = jnp.where(iota((ROWS, HD), 1) < HD // 2, -sine, sine)
+        return carry
+
     lax.fori_loop(0, 4, rope_tables, 0)
     w_copy.wait()
+    project_folded()
     second_end(0)
     project(0)
-    first_ring(3)
-    second_sends(3, 0)
     second_ring(2)
+
+    lax.fori_loop(0, NZ, pick_early, 0)
+    drain(io.at[pl.ds(0, NZ - 1)], i_recv.at[1])
+
+    @pl.when(z % 4 == 0)
+    def _():
+        drain(iox.at[pl.ds(0, 3)], ix_recv.at[1])
+
+    @pl.when(z % 4 != 0)
+    def _():
+        drain(iox.at[pl.ds(0, 4)], ix_recv.at[1])
+
+    first_sends(4)
+    second_sends(4, 0)
+    first_sends(5)
+    second_sends(5, 0)
     second_end(1)
     project(1)
     os[0, :, 0:CHUNK, :] = attend(0, 0, 2)
-    second_ring(3)
-    lax.fori_loop(0, NZ, pick_early, 0)
-    second_end(3)
-    project_folded()
+    os[0, :, CHUNK:32, :] = attend(1, 0, 2)
+    to_pieces(0)
     second_end(2)
     project(2)
     os[1, :, 0:CHUNK, :] = attend(2, 1, 3)
-    os[1, :, CHUNK:32, :] = attend(3, 2, 2)
+    behind = iota((PIECES, CHUNK, HD), 1) >= CHUNK - 2
+    os[1, :, CHUNK:32, :] = jnp.where(behind, attend(1, 1, 2), attend(3, 2, 2))
     to_pieces(1)
-
-    drain(io.at[pl.ds(0, NZ - 1)], i_recv.at[1])
-
-    @pl.when(z % 4 == 0)
-    def _():
-        drain(iox.at[pl.ds(0, 3)], ix_recv.at[1])
-
-    @pl.when(z % 4 != 0)
-    def _():
-        drain(iox.at[pl.ds(0, 4)], ix_recv.at[1])
-
-    first_sends(4)
-    second_sends(4, 0)
-    first_sends(5)
-    os[0, :, CHUNK:32, :] = attend(1, 0, 3)
-    to_pieces(0)
     first_ring(4)
+    first_ring(5)
+    share(0)
+    second_ring(4)
 
     weights = readout[...].astype(F32)
     last_row = jnp.full((1, HD), -1, I32)
@@ -449,40 +459,17 @@
         value = jnp.sum(rows.astype(F32) * weights, axis=1, keepdims=True)
         return jnp.sum(jnp.where(row == wanted, value, 0.0), axis=0, keepdims=True)
 
-    reward = jnp.zeros((1, HD), F32)
-    for k in range(2):
-        reward = reward + reward_of(os[k, PIECES - 1], 32 * k + iota((32, 1), 0), last_row)
-
-    def ring_x(i):
-        return {"tensor": y * 4 + (x + i) % 4}
-
-    def ring_y(i):
-        return {"tensor": ((y + i) % 4) * 4 + x}
-
-    def sum_start(buf, k, index, own, device_of):
-        buf[k, index] = jnp.broadcast_to(own, (8, HD))
-        for i in range(1, 4):
-            remote(buf.at[k, index], buf.at[k, index], rw_send.at[k], rw_recv.at[k], device_of(i)).start()
-
-    def sum_end(buf, k):
-        drain(buf.at[k, pl.ds(0, 3)], rw_recv.at[k])
-        return (buf[k, 0] + buf[k, 1] + buf[k, 2] + buf[k, 3])[0:1, :]
-
-    sum_start(rx, 0, x, reward, ring_x)
-    late_tables()
-    second_ring(4)
-    second_sends(5, 0)
-    first_ring(5)
-    reward = sum_end(rx, 0)
-    sum_start(rx, 1, y, reward, ring_y)
+    place = iota((32, 1), 0)
+    reward = reward_of(os[0, PIECES - 1], jnp.where(place < 30, place, -5), last_row)
+    reward = reward + reward_of(os[1, PIECES - 1], jnp.where(place < 30, 32 + place, place), last_row)
+
+    reward = reward - jnp.where(t == 0, beta_weight, 0.0) * penalty
+    sc[core, z] = jnp.broadcast_to(reward, (8, HD))
+    over_z(lambda target: remote(
+        sc.at[core, z], sc.at[core, z], rw_send.at[1], rw_recv.at[1], in_z(target)).start())
     share(1)
-    share(0)
-    reward = sum_end(rx, 1)
-    sc[core, z] = jnp.broadcast_to(reward - beta_weight * penalty, (8, HD))
-    over_z(lambda target: remote(
-        sc.at[core, z], sc.at[core, z], rw_send.at[4], rw_recv.at[4], in_z(target)).start())
+    shared(0)
     shared(1)
-    shared(0)
     src = zb[...].reshape(2 * NZ * 64, HD)
     rows = jnp.dot(sel[...].reshape(NZ * BIN_DEV, 2 * NZ * 64), src, preferred_element_type=F32)
     ob[...] = rows.astype(BF16).reshape(NZ, BIN_DEV, HD)
@@ -491,10 +478,8 @@
     fo[z] = ob[z]
 
     second_ring(5)
-    second_end(4)
-    project(4)
-    drain(sc.at[core, pl.ds(0, NZ - 1)], rw_recv.at[4])
-    sc_pass = remote(sc.at[core], sc.at[core], rw_send.at[5], rw_recv.at[5], sibling)
+    drain(sc.at[core, pl.ds(0, NZ - 1)], rw_recv.at[1])
+    sc_pass = remote(sc.at[core], sc.at[core], rw_send.at[2], rw_recv.at[2], sibling)
     sc_pass.start()
 
     seg_row = meta[core, z, 0:1, :]
@@ -502,6 +487,17 @@
     for j in range(LATE, RESP):
         upto = jnp.sum(jnp.where(seg_row <= j, 1.0, 0.0), axis=1, keepdims=True).astype(I32)
         late_last = jnp.where(lane == j, upto - 33, late_last)
+
+    second_end(4)
+    project(4)
+    remote(sc.at[1 - core], sc.at[1 - core], rw_send.at[2], rw_recv.at[2], sibling).wait_recv()
+    all_scores = sc[...].reshape(2 * NZ, 8, HD)
+    sources = jnp.full((1, HD), -1, I32)
+    for j in range(RESP):
+        sources = jnp.where(lane == j, entry_source[0:1, j:j + 1], sources)
+    mine = (tile_bin == sources.reshape(1, 1, HD)) & is_segment
+    picked = jnp.sum(jnp.where(mine, all_scores, 0.0), axis=0)
+    picked = jnp.sum(picked, axis=0, keepdims=True)
 
     second_end(5)
     project(5)
@@ -510,11 +506,11 @@
     low = jnp.concatenate([low_t[0, tail, 0:1], low_t[1, tail, 0:1]], axis=0)
     high = jnp.concatenate([high_t[0, tail, 0:1], high_t[1, tail, 0:1]], axis=0)
     last_rows = softmax_values(q_last, low, high, late_keys())
-    sum_start(rx, 2, x, reward_of(last_rows, iota((32, 1), 0), late_last), ring_x)
+    rx[t] = jnp.broadcast_to(picked + reward_of(last_rows, place, late_last), (8, HD))
+    over_plane(lambda target: remote(
+        rx.at[t], rx.at[t], rw_send.at[0], rw_recv.at[0], {"tensor": target}).start())
     late = []
     late.append(softmax_values(qs[4], low_t[0, :, 0:1], high_t[0, :, 0:1], late_keys()))
-    reward = sum_end(rx, 2)
-    sum_start(rx, 3, y, reward, ring_y)
     late.append(softmax_values(qs[5], low_t[1, :, 0:1], high_t[1, :, 0:1], late_keys()))
 
     drain(ob.at[pl.ds(0, NZ - 1)], p2_recv)
@@ -524,15 +520,6 @@
         fo[:, rows, :] = (fo[:, rows, :].astype(F32) + mine).astype(BF16)
     out_copy = pltpu.make_async_copy(fo, out, own_sem)
     out_copy.start()
-
-    remote(sc.at[1 - core], sc.at[1 - core], rw_send.at[5], rw_recv.at[5], sibling).wait_recv()
-    all_scores = sc[...].reshape(2 * NZ, 8, HD)
-    sources = jnp.full((1, HD), -1, I32)
-    for j in range(RESP):
-        sources = jnp.where(lane == j, entry_source[0:1, j:j + 1], sources)
-    mine = (tile_bin == sources.reshape(1, 1, HD)) & is_segment
-    picked = jnp.sum(jnp.where(mine, all_scores, 0.0), axis=0)
-    picked = jnp.sum(picked, axis=0, keepdims=True)
 
     for c in range(6):
         if c < 3:
@@ -562,13 +549,11 @@
     drain(ob.at[pl.ds(0, NZ - 1)], p2_send)
     drain(meta.at[core, pl.ds(0, NZ - 1)], meta_send.at[0])
     drain(meta.at[core], meta_send.at[1])
-    for k in range(3):
-        drain(rx.at[k, pl.ds(0, 3)], rw_send.at[k])
-    drain(sc.at[core, pl.ds(0, NZ - 1)], rw_send.at[4])
-    drain(sc.at[core], rw_send.at[5])
-    reward = sum_end(rx, 3)
-    scores[...] = (picked + reward)[:, 0:RESP]
-    drain(rx.at[3, pl.ds(0, 3)], rw_send.at[3])
+    drain(sc.at[core, pl.ds(0, NZ - 1)], rw_send.at[1])
+    drain(sc.at[core], rw_send.at[2])
+    drain(rx.at[pl.ds(0, PIECES - 1)], rw_recv.at[0])
+    scores[...] = jnp.sum(rx[...], axis=0)[0:1, 0:RESP]
+    drain(rx.at[pl.ds(0, PIECES - 1)], rw_send.at[0])
     out_copy.wait()
 
 
@@ -612,7 +597,7 @@
             pltpu.VMEM((NZ, BIN_DEV, 2 * NZ * 64), BF16),
             pltpu.VMEM((NZ, BIN_DEV, HD), BF16),
             pltpu.VMEM((PIECES, BIN_DEV, HD), BF16),
-            pltpu.VMEM((4, 4, 8, HD), F32),
+            pltpu.VMEM((PIECES, 8, HD), F32),
             pltpu.VMEM((2, NZ, 8, HD), F32),
             dma,
             dma((6, 4)),
@@ -630,8 +615,8 @@
             dma((4,)),
             dma,
             dma,
-            dma((6,)),
-            dma((6,)),
+            dma((3,)),
+            dma((3,)),
             dma,
         ],
         compiler_params=pltpu.CompilerParams(

time: 116 us -> 107 us (0.922)
  the two profiles are of different devices: /device:TPU:6 before, /device:TPU:11 now
where the time goes in v3:
time: 107 us
  Pallas kernels  103 us (96%)
  local copies, waits for them, and re-layouts  2.8 us (3%)
    pallas_call x1, Pallas kernels, body(): pl.pallas_call(kernel, out_shape=(jax.ShapeDtypeStruct((PIECES, BIN_DEV,...  103 us
    unnamed x2, local copies, waits for them, and re-layouts  2.8 us

profile of v3, /device:TPU:11, one launch (start us, length us, event | category | flops | bytes accessed | tf_op | source)
XLA Modules:
  0.0 106.7 jit_solution(6199428412070760091)
XLA Ops:
  0.6 103.3 %shard_map.104 = (bf16[16,64,128]{2,1,0:T(8,128)(2,1)}, f32[1,8]{1,0:T(1,128)}) custom-call(bf16[80,4608]{1,0:T(8,128)(2,1)} %bitcast.6, bf16[8,160]{1,0:T(8,128)(2,1)} %bitcast.9, f32[36,128]{1,0:T(8,128)} %bitcast.8, f32[1,128]{1,0:T(1,128)} %constant.2.clone.freq, bf16[4608,384]{1,0:T(8,128)(2,1)} %bitcast.5, bf16[1,128]{1,0:T(2,128)(2,1)} %readout.1, ...), custom_call_target="tpu_custom_call" | custom-call | tf_op jit(solution)/shard_map/pallas_call | solution.py:567
  103.9 1.7 %copy.13 = bf16[1,1024,128]{2,1,0:T(8,128)(2,1)} copy(bf16[1,1024,128]{2,1,0:T(8,128)(2,1)} %bitcast.7) | data formatting | bytes 524288
  105.6 1.1 %copy.14 = f32[1,8]{1,0:T(1,128)} copy(f32[1,8]{1,0:T(1,128)} %get-tuple-element.9) | data formatting | bytes 64

commit v4 on v3

--- a/solution.py
+++ b/solution.py
@@ -55,7 +55,7 @@
     resp, kl, gain, freq, w_hbm, readout, slot_bin, entry_source, bin_segments,
     out, scores,
     ge, gx, gl, nb, w, meta, cos_t, sin_t, low_t, high_t, code_t, qs, ks, vs,
-    ib, ibx, io, iox, seli, os, zb, sel, ob, fo, rx, sc,
+    ib, ibx, io, iox, seli, os, zb, sel0, sel, ob0, ob, fo, rx, sc,
     w_sem, r1, r2, ag_send, meta_send, meta_recv, i_send, i_recv, ix_send, ix_recv,
     p1_send, p1_recv, sib_send, sib_recv, p2_send, p2_recv, rw_send, rw_recv, own_sem,
 ):
@@ -188,21 +188,28 @@
             half(c, opposite, 0, r2.at[c, i, 2], up_b).wait_recv()
             half(c, opposite, 1, r2.at[c, i, 3], down_b).wait_recv()
 
-    def main_cols(target):
-        return pl.ds(pl.multiple_of(target * MAIN, MAIN), MAIN)
+    def half_cols(target, h):
+        return pl.ds(pl.multiple_of(target * MAIN + h * EXTRA, EXTRA), EXTRA)
 
     def extra_cols(target):
         return pl.ds(pl.multiple_of(NZ * MAIN + (target // 4) * EXTRA, EXTRA), EXTRA)
 
-    def spread(target):
-        remote(nb.at[:, main_cols(target)], ib.at[core, z], i_send.at[0], i_recv.at[0], in_z(target)).start()
+    def spread(target, h):
+        remote(nb.at[:, half_cols(target, h)], ib.at[h, core, z], i_send.at[h], i_recv.at[h], in_z(target)).start()
+
+    def spread_extra(target):
+        spread(target, 1)
 
         @pl.when(target % 4 == 0)
         def _():
             remote(nb.at[:, extra_cols(target)], ibx.at[core, z], ix_send.at[0], ix_recv.at[0], in_z(target)).start()
 
-    def collect(target):
-        remote(io.at[target], gl.at[t, :, main_cols(z)], i_send.at[1], i_recv.at[1], in_z(target)).start()
+    def collect(target, h):
+        remote(
+            io.at[h, target], gl.at[t, :, half_cols(z, h)], i_send.at[2 + h], i_recv.at[2 + h], in_z(target)).start()
+
+    def collect_extra(target):
+        collect(target, 1)
 
         @pl.when(z % 4 == 0)
         def _():
@@ -212,13 +219,15 @@
     second_sends(3, 0)
     first_sends(0)
     second_sends(0, 0)
-    over_z(spread)
+    over_z(lambda target: spread(target, 0))
     first_sends(1)
     second_sends(1, 0)
     over_z(lambda target: remote(
         meta.at[core, z], meta.at[core, z], meta_send.at[0], meta_recv.at[0], in_z(target)).start())
     first_sends(2)
-    ib[core, z] = nb[:, main_cols(z)]
+    over_z(spread_extra)
+    for h in range(2):
+        ib[h, core, z] = nb[:, half_cols(z, h)]
 
     @pl.when(z % 4 == 0)
     def _():
@@ -228,7 +237,6 @@
     first_ring(0)
     second_sends(2, 0)
     second_ring(3)
-    first_ring(1)
 
     drain(meta.at[core, pl.ds(0, NZ - 1)], meta_recv.at[0])
     meta_pass = remote(meta.at[core], meta.at[core], meta_send.at[1], meta_recv.at[1], sibling)
@@ -273,39 +281,51 @@
             code = jnp.where(live, slot * LMAX + position, 2.0 * RESP * LMAX)
             code_t[c] = jnp.transpose(code)[0:8, :]
 
-    late_tables()
     def pick_early(i, carry):
         seg, _, within, place = bin_rows(meta[core, i], 0, BIN_DEV)
         row = CAP * seg.astype(I32) + within.astype(I32)
-        column = place * 32 + jnp.where(row < 30, row, 2 * NZ * 32 + jnp.where(row < 32, row, row - 32))
-        column = jnp.where(seg < LATE, column, -1)
-        sel[i] = jnp.where(iota((BIN_DEV, 2 * NZ * 64), 1) == column, 1.0, 0.0).astype(BF16)
+        first = jnp.where((seg < LATE) & (row < 30), place * 32 + row, -1)
+        second = jnp.where((seg < LATE) & (row >= 30), place * 32 + jnp.where(row < 32, row, row - 32), -1)
+        spot = iota((BIN_DEV, 2 * NZ * 32), 1)
+        sel0[i] = jnp.where(spot[0:32] == first[0:32], 1.0, 0.0).astype(BF16)
+        sel[i] = jnp.where(spot == second, 1.0, 0.0).astype(BF16)
         return carry
 
+    def pass_on(h):
+        drain(ib.at[h, core, pl.ds(0, NZ - 1)], i_recv.at[h])
+        remote(ib.at[h, core], ib.at[h, core], sib_send.at[2 + h], sib_recv.at[2 + h], sibling).start()
+
+    def choose(h):
+        remote(ib.at[h, 1 - core], ib.at[h, 1 - core], sib_send.at[2 + h], sib_recv.at[2 + h], sibling).wait_recv()
+        picks = seli[...].reshape(NZ * 32, 2 * NZ * 32)
+        rows = jnp.dot(picks, ib[h].reshape(2 * NZ * 32, EXTRA), preferred_element_type=F32)
+        io[h] = rows.astype(BF16).reshape(NZ, 32, EXTRA)
+
     lax.fori_loop(0, NZ, pick_late, 0)
-    drain(ib.at[core, pl.ds(0, NZ - 1)], i_recv.at[0])
-    ib_pass = remote(ib.at[core], ib.at[core], sib_send.at[2], sib_recv.at[2], sibling)
-    ib_pass.start()
+    pass_on(0)
+    first_ring(1)
+    choose(0)
+    over_z(lambda target: collect(target, 0))
+    pass_on(1)
 
     @pl.when(z % 4 == 0)
     def _():
         drain(ibx.at[core, pl.ds(0, NZ - 1)], ix_recv.at[0])
-        remote(ibx.at[core], ibx.at[core], sib_send.at[3], sib_recv.at[3], sibling).start()
+        remote(ibx.at[core], ibx.at[core], sib_send.at[4], sib_recv.at[4], sibling).start()
 
     second_ring(0)
-    remote(ib.at[1 - core], ib.at[1 - core], sib_send.at[2], sib_recv.at[2], sibling).wait_recv()
-    picks = seli[...].reshape(NZ * 32, 2 * NZ * 32)
-    rows = jnp.dot(picks, ib[...].reshape(2 * NZ * 32, MAIN), preferred_element_type=F32)
-    io[...] = rows.astype(BF16).reshape(NZ, 32, MAIN)
+    choose(1)
 
     @pl.when(z % 4 == 0)
     def _():
-        remote(ibx.at[1 - core], ibx.at[1 - core], sib_send.at[3], sib_recv.at[3], sibling).wait_recv()
+        remote(ibx.at[1 - core], ibx.at[1 - core], sib_send.at[4], sib_recv.at[4], sibling).wait_recv()
+        picks = seli[...].reshape(NZ * 32, 2 * NZ * 32)
         rows = jnp.dot(picks, ibx[...].reshape(2 * NZ * 32, EXTRA), preferred_element_type=F32)
         iox[...] = rows.astype(BF16).reshape(NZ, 32, EXTRA)
 
-    over_z(collect)
-    gl[t, :, main_cols(z)] = io[z]
+    over_z(collect_extra)
+    for h in range(2):
+        gl[t, :, half_cols(z, h)] = io[h, z]
 
     @pl.when(z % 4 == 0)
     def _():
@@ -352,9 +372,10 @@
             result = result + jnp.dot((e * inverse).astype(BF16), vs[ck], preferred_element_type=F32)
         return result.astype(BF16)
 
-    def attend(cq, first, count):
+    in_chunk = iota((ROWS, 1), 0) % CHUNK
+
+    def attend(q, row, first, count):
         index = iota((ROWS, 1), 0)
-        row = CHUNK * cq + index % CHUNK
         slot = slot_of(row)
         low = slot * LMAX
         high = low + (index // CHUNK) * CAP + row - CAP * slot
@@ -367,7 +388,7 @@
             code = kslot * LMAX + (kidx // CHUNK) * CAP + within
             live = (within < per_slot(kslot, counts)) & (kslot < LATE)
             keys.append((ck, jnp.where(live, code, 2 * RESP * LMAX)))
-        return softmax_values(qs[cq], low, high, keys).reshape(PIECES, CHUNK, HD)
+        return softmax_values(q, low, high, keys).reshape(PIECES, CHUNK, HD)
 
     def to_pieces(k):
         over_z(lambda target: remote(
@@ -409,13 +430,15 @@
 
     lax.fori_loop(0, 4, rope_tables, 0)
     w_copy.wait()
+    late_tables()
     project_folded()
     second_end(0)
     project(0)
     second_ring(2)
 
     lax.fori_loop(0, NZ, pick_early, 0)
-    drain(io.at[pl.ds(0, NZ - 1)], i_recv.at[1])
+    for h in range(2):
+        drain(io.at[h, pl.ds(0, NZ - 1)], i_recv.at[2 + h])
 
     @pl.when(z % 4 == 0)
     def _():
@@ -431,14 +454,16 @@
     second_sends(5, 0)
     second_end(1)
     project(1)
-    os[0, :, 0:CHUNK, :] = attend(0, 0, 2)
-    os[0, :, CHUNK:32, :] = attend(1, 0, 2)
+    os[0, :, 0:CHUNK, :] = attend(qs[0], in_chunk, 0, 2)
+    os[0, :, CHUNK:32, :] = attend(qs[1], CHUNK + in_chunk, 0, 2)
     to_pieces(0)
     second_end(2)
     project(2)
-    os[1, :, 0:CHUNK, :] = attend(2, 1, 3)
-    behind = iota((PIECES, CHUNK, HD), 1) >= CHUNK - 2
-    os[1, :, CHUNK:32, :] = jnp.where(behind, attend(1, 1, 2), attend(3, 2, 2))
+    os[1, :, 0:CHUNK, :] = attend(qs[2], 2 * CHUNK + in_chunk, 1, 3)
+    behind = in_chunk >= CHUNK - 2
+    mixed = jnp.where(behind, qs[1].astype(F32), qs[3].astype(F32)).astype(BF16)
+    row = in_chunk + jnp.where(behind, CHUNK, 3 * CHUNK)
+    os[1, :, CHUNK:32, :] = attend(mixed, row, 1, 3)
     to_pieces(1)
     first_ring(4)
     first_ring(5)
@@ -467,12 +492,17 @@
     sc[core, z] = jnp.broadcast_to(reward, (8, HD))
     over_z(lambda target: remote(
         sc.at[core, z], sc.at[core, z], rw_send.at[1], rw_recv.at[1], in_z(target)).start())
+    shared(0)
+    src = zb[0].reshape(2 * NZ * 32, HD)
+    rows = jnp.dot(sel0[...].reshape(NZ * 32, 2 * NZ * 32), src, preferred_element_type=F32)
+    ob0[...] = rows.reshape(NZ, 32, HD)
     share(1)
-    shared(0)
     shared(1)
-    src = zb[...].reshape(2 * NZ * 64, HD)
-    rows = jnp.dot(sel[...].reshape(NZ * BIN_DEV, 2 * NZ * 64), src, preferred_element_type=F32)
-    ob[...] = rows.astype(BF16).reshape(NZ, BIN_DEV, HD)
+    src = zb[1].reshape(2 * NZ * 32, HD)
+    rows = jnp.dot(sel[...].reshape(NZ * BIN_DEV, 2 * NZ * 32), src, preferred_element_type=F32)
+    rows = rows.reshape(NZ, BIN_DEV, HD)
+    ob[:, 0:32, :] = (rows[:, 0:32] + ob0[...]).astype(BF16)
+    ob[:, 32:64, :] = rows[:, 32:64].astype(BF16)
     over_z(lambda target: remote(
         ob.at[target], fo.at[z], p2_send, p2_recv, in_z(target)).start())
     fo[z] = ob[z]
@@ -529,14 +559,14 @@
         else:
             sent = gl.at[pl.ds(0, 15), pl.ds(CHUNK * (c - 4), CHUNK)]
         drain(sent, ag_send.at[c])
-    drain(io.at[pl.ds(0, NZ - 1)], i_send.at[0])
-    drain(io.at[pl.ds(0, NZ - 1)], i_send.at[1])
+    for h in range(4):
+        drain(io.at[0, pl.ds(0, NZ - 1)], i_send.at[h])
 
     @pl.when(z % 4 == 0)
     def _():
         drain(iox.at[pl.ds(0, 3)], ix_send.at[0])
         drain(iox.at[pl.ds(0, NZ - 1)], ix_send.at[1])
-        drain(ibx.at[core], sib_send.at[3])
+        drain(ibx.at[core], sib_send.at[4])
 
     @pl.when(z % 4 != 0)
     def _():
@@ -545,7 +575,8 @@
     for k in range(2):
         drain(os.at[k, pl.ds(0, NZ - 1)], p1_send.at[k])
         drain(zb.at[k, core], sib_send.at[k])
-    drain(ib.at[core], sib_send.at[2])
+    for h in range(2):
+        drain(ib.at[h, core], sib_send.at[2 + h])
     drain(ob.at[pl.ds(0, NZ - 1)], p2_send)
     drain(meta.at[core, pl.ds(0, NZ - 1)], meta_send.at[0])
     drain(meta.at[core], meta_send.at[1])
@@ -587,14 +618,16 @@
             pltpu.VMEM((6, ROWS, HD), BF16),
             pltpu.VMEM((6, ROWS, HD), BF16),
             pltpu.VMEM((6, ROWS, HD), BF16),
-            pltpu.VMEM((2, NZ, 32, MAIN), BF16),
+            pltpu.VMEM((2, 2, NZ, 32, EXTRA), BF16),
             pltpu.VMEM((2, NZ, 32, EXTRA), BF16),
-            pltpu.VMEM((NZ, 32, MAIN), BF16),
+            pltpu.VMEM((2, NZ, 32, EXTRA), BF16),
             pltpu.VMEM((NZ, 32, EXTRA), BF16),
             pltpu.VMEM((NZ, 32, 2 * NZ * 32), BF16),
             pltpu.VMEM((2, PIECES, 32, HD), BF16),
             pltpu.VMEM((2, 2, NZ, 32, HD), BF16),
-            pltpu.VMEM((NZ, BIN_DEV, 2 * NZ * 64), BF16),
+            pltpu.VMEM((NZ, 32, 2 * NZ * 32), BF16),
+            pltpu.VMEM((NZ, BIN_DEV, 2 * NZ * 32), BF16),
+            pltpu.VMEM((NZ, 32, HD), F32),
             pltpu.VMEM((NZ, BIN_DEV, HD), BF16),
             pltpu.VMEM((PIECES, BIN_DEV, HD), BF16),
             pltpu.VMEM((PIECES, 8, HD), F32),
@@ -605,14 +638,14 @@
             dma((6,)),
             dma((2,)),
             dma((2,)),
+            dma((4,)),
+            dma((4,)),
             dma((2,)),
             dma((2,)),
             dma((2,)),
             dma((2,)),
-            dma((2,)),
-            dma((2,)),
-            dma((4,)),
-            dma((4,)),
+            dma((5,)),
+            dma((5,)),
             dma,
             dma,
             dma((3,)),

time: 107 us -> 105 us (0.981)
  the two profiles are of different devices: /device:TPU:11 before, /device:TPU:6 now
where the time goes in v4:
time: 105 us
  Pallas kernels  101 us (96%)
  local copies, waits for them, and re-layouts  2.8 us (3%)
    pallas_call x1, Pallas kernels, body(): pl.pallas_call(kernel, out_shape=(jax.ShapeDtypeStruct((PIECES, BIN_DEV,...  101 us
    unnamed x2, local copies, waits for them, and re-layouts  2.8 us

profile of v4, /device:TPU:6, one launch (start us, length us, event | category | flops | bytes accessed | tf_op | source)
XLA Modules:
  0.0 104.9 jit_solution(9419408582646860474)
XLA Ops:
  0.6 101.4 %shard_map.104 = (bf16[16,64,128]{2,1,0:T(8,128)(2,1)}, f32[1,8]{1,0:T(1,128)}) custom-call(bf16[80,4608]{1,0:T(8,128)(2,1)} %bitcast.6, bf16[8,160]{1,0:T(8,128)(2,1)} %bitcast.9, f32[36,128]{1,0:T(8,128)} %bitcast.8, f32[1,128]{1,0:T(1,128)} %constant.2.clone.freq, bf16[4608,384]{1,0:T(8,128)(2,1)} %bitcast.5, bf16[1,128]{1,0:T(2,128)(2,1)} %readout.1, ...), custom_call_target="tpu_custom_call" | custom-call | tf_op jit(solution)/shard_map/pallas_call | solution.py:598
  102.1 1.7 %copy.13 = bf16[1,1024,128]{2,1,0:T(8,128)(2,1)} copy(bf16[1,1024,128]{2,1,0:T(8,128)(2,1)} %bitcast.7) | data formatting | bytes 524288
  103.7 1.1 %copy.14 = f32[1,8]{1,0:T(1,128)} copy(f32[1,8]{1,0:T(1,128)} %get-tuple-element.9) | data formatting | bytes 64
